TPU v7x, 128 devices: a whole 4x4x4 slice. The times are simulated.
128 devices in a mesh: grp: 8 (over z_lo, y), mem: 16 (over z_hi, x, core).
Axes of the slice: x: 4, y: 4, z: 4 (z_hi: 2, z_lo: 2; z = z_hi * 2 + z_lo), core: 2. Of those that a mesh axis runs over, the one named last changes fastest.
Arguments:
- fine_rows: bfloat16 [24576, 768], P(('grp', 'mem')), may hold values from -6 to 6
- coarse_rows: bfloat16 [24576, 768], P(('grp', 'mem')), may hold values from -6 to 6
- fine_head: bfloat16 [768, 768], replicated, may hold values from -0.0078125 to 0.0078125
- coarse_head: bfloat16 [768, 768], replicated, may hold values from -0.0078125 to 0.0078125
- log_scale: float32 [1], replicated, may hold values from 1.5 to 2.5
- bias: float32 [1], replicated, may hold values from -6 to -3
Outputs:
- loss: float32 [1], replicated
- fine_grad: float32 [24576, 768], P(('grp', 'mem'))
- coarse_grad: float32 [24576, 768], P(('grp', 'mem'))
- fine_head_grad: float32 [768, 768], replicated
- coarse_head_grad: float32 [768, 768], replicated
All inputs are finite; a program needn't handle non-finite values.
Results may differ from a plain program's by a relative error of at most 0.02.
Values may be sent and summed in bfloat16 or wider, within the bound.
A program may use at most 128 MiB of HBM per device.

v0:
```python
import jax
import jax.numpy as jnp
from jax import lax
from jax.sharding import PartitionSpec as P

EPS = 1e-06


def embed(rows, weight):
    proj = jnp.dot(rows, weight, preferred_element_type=jnp.float32)
    inv = lax.rsqrt(jnp.sum(proj * proj, axis=-1, keepdims=True) + EPS)
    return (proj * inv, inv)


def head_back(unit, inv, grad_unit):
    inner = jnp.sum(unit * grad_unit, axis=-1, keepdims=True)
    return (inv * (grad_unit - unit * inner)).astype(jnp.bfloat16)


def pair_tile(rows_part, cols_part, row_ids, col_ids, scale, shift):
    sign = jnp.where(row_ids[:, None] == col_ids[None, :], 1.0, -1.0).astype(jnp.float32)
    logit = (
        scale
        * lax.dot_general(
            rows_part, cols_part, (((1,), (1,)), ((), ())), preferred_element_type=jnp.float32
        )
        + shift
    )
    margin = sign * logit
    part_total = jnp.sum(jax.nn.softplus(-margin))
    coef = (-sign * jax.nn.sigmoid(-margin) * scale).astype(jnp.bfloat16)
    row_part = jnp.dot(coef, cols_part, preferred_element_type=jnp.float32)
    col_part = lax.dot_general(
        coef, rows_part, (((0,), (0,)), ((), ())), preferred_element_type=jnp.float32
    )
    return (row_part, col_part, part_total)


def shards(fine_rows, coarse_rows, fine_head, coarse_head, log_scale, bias):
    rows = fine_rows.shape[0]
    n_mem = lax.axis_size("mem")
    n_grp = lax.axis_size("grp")
    group = lax.axis_index("grp")
    member = lax.axis_index("mem")
    fine_unit, fine_inv = embed(fine_rows, fine_head)
    coarse_unit, coarse_inv = embed(coarse_rows, coarse_head)
    fine_emb = fine_unit.astype(jnp.bfloat16)
    coarse_emb = coarse_unit.astype(jnp.bfloat16)
    scale = jnp.exp(log_scale[0])
    shift = bias[0]
    rows_block = lax.all_gather(fine_emb, "mem", axis=0, tiled=True)
    row_ids = group * n_mem * rows + jnp.arange(n_mem * rows, dtype=jnp.int32)
    piece = lax.all_gather(coarse_emb, "grp", axis=0, tiled=True)
    position = jnp.arange(piece.shape[0], dtype=jnp.int32)
    col_ids = (position // rows * n_mem + member) * rows + position % rows
    row_part, col_part, part_total = pair_tile(rows_block, piece, row_ids, col_ids, scale, shift)
    acc_cols = col_part
    acc_rows, acc_cols, total = (row_part, acc_cols, part_total)
    fine_dz = lax.psum_scatter(
        acc_rows.astype(jnp.bfloat16), "mem", scatter_dimension=0, tiled=True
    ).astype(jnp.float32)
    coarse_dz = lax.psum_scatter(
        acc_cols.astype(jnp.bfloat16), "grp", scatter_dimension=0, tiled=True
    ).astype(jnp.float32)
    fine_dp = head_back(fine_unit, fine_inv, fine_dz)
    coarse_dp = head_back(coarse_unit, coarse_inv, coarse_dz)
    dims = (((1,), (1,)), ((), ()))
    fine_grad = lax.dot_general(fine_dp, fine_head, dims, preferred_element_type=jnp.float32)
    coarse_grad = lax.dot_general(coarse_dp, coarse_head, dims, preferred_element_type=jnp.float32)
    outer = (((0,), (0,)), ((), ()))
    fine_part = lax.dot_general(fine_rows, fine_dp, outer, preferred_element_type=jnp.float32)
    coarse_part = lax.dot_general(coarse_rows, coarse_dp, outer, preferred_element_type=jnp.float32)
    fine_head_grad, coarse_head_grad, summed = lax.psum(
        (fine_part, coarse_part, total), ("grp", "mem")
    )
    pairs = rows * n_mem * n_grp
    loss = jnp.reshape(summed / (pairs * pairs), (1,))
    return (loss, fine_grad, coarse_grad, fine_head_grad, coarse_head_grad)


def solution(mesh):
    placed = (P(("grp", "mem"), None), P(("grp", "mem"), None), P(), P(), P(), P())
    return jax.shard_map(
        shards,
        mesh=mesh,
        in_specs=placed,
        out_specs=(P(), P(("grp", "mem"), None), P(("grp", "mem"), None), P(), P()),
        check_vma=False,
    )
```

profile of v0, /device:TPU:1, one launch (start us, length us, event | category | flops | bytes accessed | tf_op | source)
XLA Modules:
  0.0 458.2 jit_solution(3634196277997558784)
XLA Ops:
  7.2 0.0 copy-start
  7.2 0.0 all-gather.5.cloned.1.call-start
  7.2 1.2 copy-done
  8.4 1.5 multiply_reduce_fusion
  9.9 0.8 multiply_convert_fusion
  10.7 0.0 all-gather.5.cloned.1.call-update
  10.8 0.0 all-gather.3.cloned.1.call-start
  10.8 1.9 multiply_reduce_fusion.1
  12.7 0.8 multiply_convert_fusion.1
  13.5 0.0 all-gather.3.cloned.1.call-update
  13.5 0.0 reduce-scatter.5.cloned.1.call-start
  15.0 36.3 %all-gather.5.cloned.1.call-done = bf16[1536,768]{1,0:T(8,128)(2,1)} async-done(((bf16[192,768]{1,0:T(8,128)(2,1)}), bf16[1536,768]{1,0:T(8,128)(2,1)}) %all-gather.5.cloned.1.call-update) | async-done | bytes 2359312 | tf_op jit(solution)/shard_map/all_gather | solution.py:53
  51.3 65.5 %all-gather.3.cloned.1.call-done = bf16[3072,768]{1,0:T(8,128)(2,1)} async-done(((bf16[192,768]{1,0:T(8,128)(2,1)}), bf16[3072,768]{1,0:T(8,128)(2,1)}) %all-gather.3.cloned.1.call-update) | async-done | bytes 4718608 | tf_op jit(solution)/shard_map/all_gather | solution.py:51
  116.8 0.0 copy-start.5
  116.8 27.4 %fusion.2 = (bf16[3072,1536]{1,0:T(8,128)(2,1)S(1)}, f32[]{:T(128)}) fusion(f32[]{:T(128)} %bitcast, s32[1536]{0:T(1024)S(1)} %fusion.19, s32[3072]{0:T(1024)S(1)} %iota_add_fusion, f32[]{:T(128)} %bitcast.25, bf16[3072,768]{1,0:T(8,128)(2,1)} %all-gather.3.cloned.1.call-done, bf16[1536,768]{1,0:T(8,128)(2,1)} %all-gather.5.cloned.1.call-done), kind=kOutput, calls=%fused_computation.5 | convolution fusion | flops 7337410560 | bytes 16533516 | tf_op jit(solution)/shard_map/dot_general | solution.py:24
  144.2 0.0 copy-start.6
  144.2 3.6 copy-done.6
  147.8 0.0 copy-done.5
  147.8 9.0 %convolution_convert_fusion.1 = bf16[1536,768]{1,0:T(8,128)(2,1)} fusion(bf16[3072,1536]{1,0:T(8,128)(2,1)S(1)} %get-tuple-element.12, bf16[3072,768]{1,0:T(8,128)(2,1)S(1)} %copy-done.5), kind=kOutput, calls=%fused_computation.8 | convolution fusion | flops 7248936960 | bytes 16515072 | tf_op jit(solution)/shard_map/dot_general | solution.py:33
  156.8 0.0 reduce-scatter.5.cloned.1.call-update
  156.8 0.2 reduce-scatter.3.cloned.1.call-start
  157.0 12.3 %convolution_convert_fusion = bf16[3072,768]{1,0:T(8,128)(2,1)} fusion(bf16[3072,1536]{1,0:T(8,128)(2,1)} %copy-done.6, bf16[1536,768]{1,0:T(8,128)(2,1)} %all-gather.5.cloned.1.call-done), kind=kOutput, calls=%fused_computation.7 | convolution fusion | flops 7250116608 | bytes 16515072 | tf_op jit(solution)/shard_map/dot_general | solution.py:32
  169.4 0.0 copy-start.3
  169.4 0.0 reduce-scatter.3.cloned.1.call-update
  169.4 0.0 copy-start.4
  169.4 0.0 all-reduce.3.cloned.1.call-start
  169.5 24.2 %reduce-scatter.5.cloned.1.call-done = bf16[192,768]{1,0:T(8,128)(2,1)} async-done(((bf16[1536,768]{1,0:T(8,128)(2,1)}), bf16[192,768]{1,0:T(8,128)(2,1)}) %reduce-scatter.5.cloned.1.call-update) | async-done | bytes 294928 | tf_op jit(solution)/shard_map/reduce_scatter | solution.py:62
  193.6 1.2 fusion.7
  194.8 1.1 fusion.9
  196.0 0.0 copy-done.3
  196.0 1.9 convolution_bitcast_fusion
  197.9 85.7 %reduce-scatter.3.cloned.1.call-done = bf16[192,768]{1,0:T(8,128)(2,1)} async-done(((bf16[3072,768]{1,0:T(8,128)(2,1)}), bf16[192,768]{1,0:T(8,128)(2,1)}) %reduce-scatter.3.cloned.1.call-update) | async-done | bytes 294928 | tf_op jit(solution)/shard_map/reduce_scatter | solution.py:59
  283.6 1.2 fusion.4
  284.8 1.1 fusion.6
  286.0 0.0 copy-done.4
  286.0 0.0 copy-start.1
  286.0 1.9 convolution_bitcast_fusion.1
  287.9 0.0 all-reduce.3.cloned.1.call-update
  288.0 65.5 %psum.21 = f32[]{:T(128)} all-reduce(f32[]{:T(128)} %get-tuple-element.13), channel_id=1, replica_groups=mesh['grp'=8,'mem'=16] {'grp','mem'}, use_global_device_ids=true, to_apply=%region_3.4 | all-reduce | flops 1 | bytes 8 | tf_op jit(solution)/shard_map/psum | solution.py:73
  354.1 1.4 fusion.22
  355.5 0.0 copy-done.1
  355.5 1.4 fusion.21
  356.9 88.5 %all-reduce.3.cloned.1.call-done = (f32[768,768]{0,1:T(8,128)}, f32[768,768]{0,1:T(8,128)}) async-done(((f32[768,768]{0,1:T(8,128)}, f32[768,768]{0,1:T(8,128)}), (f32[768,768]{0,1:T(8,128)}, f32[768,768]{0,1:T(8,128)})) %all-reduce.3.cloned.1.call-update) | async-done | bytes 4718608 | tf_op jit(solution)/shard_map/psum | solution.py:73
  445.4 0.0 copy-start.2
  445.4 3.2 copy.11
  448.6 0.0 copy-done.2
  448.6 1.9 copy.12
  (4 shorter events, 0.0 us)
Async XLA Ops:
  7.2 1.3 copy-start
  7.2 44.1 %all-gather.5.cloned.1.call-start = ((), (), s32[]{:S(2)}) async-start(), calls=%async_computation.3 | async-start | bytes 2654208 | tf_op jit(solution)/shard_map/all_gather | solution.py:53
  10.8 106.0 %all-gather.3.cloned.1.call-start = ((), (), s32[]{:S(2)}) async-start(), calls=%async_computation.2 | async-start | bytes 5013504 | tf_op jit(solution)/shard_map/all_gather | solution.py:51
  13.5 180.1 %reduce-scatter.5.cloned.1.call-start = ((), (), s32[]{:S(2)}) async-start(), calls=%async_computation.5 | async-start | bytes 2654208 | tf_op jit(solution)/shard_map/reduce_scatter | solution.py:62
  116.8 31.0 %copy-start.5 = (bf16[3072,768]{1,0:T(8,128)(2,1)S(1)}, bf16[3072,768]{1,0:T(8,128)(2,1)}, u32[]{:S(2)}) copy-start(bf16[3072,768]{1,0:T(8,128)(2,1)} %all-gather.3.cloned.1.call-done) | copy-start | bytes 14155780
  144.2 3.6 copy-start.6
  156.8 126.8 %reduce-scatter.3.cloned.1.call-start = ((), (), s32[]{:S(2)}) async-start(), calls=%async_computation.4 | async-start | bytes 5013504 | tf_op jit(solution)/shard_map/reduce_scatter | solution.py:59
  169.4 26.6 %copy-start.3 = (bf16[192,768]{1,0:T(8,128)(2,1)S(1)}, bf16[192,768]{1,0:T(8,128)(2,1)}, u32[]{:S(2)}) copy-start(bf16[192,768]{1,0:T(8,128)(2,1)} %param.7) | copy-start | bytes 884740
  169.4 116.6 %copy-start.4 = (bf16[192,768]{1,0:T(8,128)(2,1)S(1)}, bf16[192,768]{1,0:T(8,128)(2,1)}, u32[]{:S(2)}) copy-start(bf16[192,768]{1,0:T(8,128)(2,1)} %param.6) | copy-start | bytes 884740
  169.4 276.0 %all-reduce.3.cloned.1.call-start = ((), (), s32[]{:S(2)}) async-start(), calls=%async_computation.6 | async-start | bytes 9437184 | tf_op jit(solution)/shard_map/psum | solution.py:73
  286.0 69.5 %copy-start.1 = (bf16[768,768]{1,0:T(8,128)(2,1)S(1)}, bf16[768,768]{1,0:T(8,128)(2,1)}, u32[]{:S(2)}) copy-start(bf16[768,768]{1,0:T(8,128)(2,1)} %param.8) | copy-start | bytes 3538948
  445.4 3.2 copy-start.2
Sparse Core Ops, SparseCore 0:
  10.9 40.3 all-gather.4
  54.3 62.4 all-gather.2
  156.9 36.6 reduce-scatter.4
  197.6 86.0 reduce-scatter.2
  289.9 155.4 all-reduce.2
where the time goes:
time: 459 us; the launch traced here: 458 us
  waiting for transfers between devices  300 us (65%)
  blocking collectives  65.5 us (14%)
  matrix products  58.7 us (13%)
  between operations  17 us (4%)
  local copies, waits for them, and re-layouts  10 us (2%)
  other arithmetic  6.34 us (1%)
    psum x1, waiting for transfers between devices, shards(): lax.psum((fine_part, coarse_part, total), ('grp', 'mem'))  88.5 us
    reduce_scatter x1, waiting for transfers between devices, shards(): lax.psum_scatter(acc_rows.astype(jnp.bfloat16), 'mem', scatter_dimension=...  85.7 us
    psum x1, blocking collectives, shards(): lax.psum((fine_part, coarse_part, total), ('grp', 'mem'))  65.5 us
    all_gather x1, waiting for transfers between devices, shards(): rows_block = lax.all_gather(fine_emb, 'mem', axis=0, tiled=True)  65.5 us
    all_gather x1, waiting for transfers between devices, shards(): piece = lax.all_gather(coarse_emb, 'grp', axis=0, tiled=True)  36.3 us
    dot_general x1, matrix products, pair_tile(): lax.dot_general(rows_part, cols_part, (((1,), (1,)), ((), ())), preferred...  27.4 us
    reduce_scatter x1, waiting for transfers between devices, shards(): lax.psum_scatter(acc_cols.astype(jnp.bfloat16), 'grp', scatter_dimension=...  24.2 us
    dot_general x1, matrix products, pair_tile(): row_part = jnp.dot(coef, cols_part, preferred_element_type=jnp.float32)  12.3 us
  transfers between devices with their start and end apart: 5, of which 5 were waited for; matrix products, arithmetic and copies ran while one was open for 5% of the time, Pallas kernels for 0%

commit v1 on v0

v1 whole, which is shorter than its diff:
```python
import jax
import jax.numpy as jnp
from jax import lax
from jax.experimental import pallas as pl
from jax.experimental.pallas import tpu as pltpu
from jax.sharding import PartitionSpec as P

MESH = pl.DeviceIdType.MESH
EPS = 1e-06
F32 = jnp.float32
BF16 = jnp.bfloat16
VMEM = pltpu.VMEM


def dot(a, b, dims):
    return lax.dot_general(a, b, (dims, ((), ())), preferred_element_type=F32)


NN = ((1,), (0,))
NT = ((1,), (1,))
TN = ((0,), (0,))


class Place:
    def __init__(self):
        grp, mem = lax.axis_index("grp"), lax.axis_index("mem")
        self.core = mem % 2
        self.x, self.y = (mem // 2) % 4, grp % 4
        self.z = (mem // 8) * 2 + grp // 4
        self.steps = {("x", d): self.at(dx=d) for d in (1, 2, 3)}
        self.steps |= {("y", d): self.at(dy=d) for d in (1, 2, 3)}
        self.steps |= {("z", d): self.at(z=(self.z + d) % 4) for d in (1, 2, 3)}
        self.sibling = self.at(core=1 - self.core)
        self.other_hi = self.steps["z", 2]
        self.other_lo = self.at(z=self.z + 1 - 2 * (self.z % 2))

    def at(self, dx=0, dy=0, z=None, core=None):
        x, y = (self.x + dx) % 4, (self.y + dy) % 4
        z = self.z if z is None else z
        core = self.core if core is None else core
        return ((z % 2) * 4 + y, (z // 2) * 8 + x * 2 + core)

    def along(self, axis, step):
        return self.steps[axis, step]


def view(ref, *index):
    return ref.at[index] if index else ref


class Copies:
    def __init__(self, send_sem, recv_sem):
        self.send_sem, self.recv_sem = send_sem, recv_sem
        self.made = {}

    def start(self, name, src, dst, device):
        index = len(self.made)
        assert name not in self.made and index < N_COPIES

        def make():
            return pltpu.make_async_remote_copy(
                src_ref=view(*src),
                dst_ref=view(*dst),
                send_sem=self.send_sem.at[index],
                recv_sem=self.recv_sem.at[index],
                device_id=device,
                device_id_type=MESH,
            )

        self.made[name] = make
        make().start()

    def wait(self, *names):
        for name in names:
            self.made[name]().wait_recv()

    def finish(self):
        for make in self.made.values():
            make().wait_send()


N_COPIES = 96


def kernel(
    fine_rows,
    coarse_rows,
    fine_head,
    coarse_head,
    log_scale,
    bias,
    loss_out,
    fine_grad,
    coarse_grad,
    fine_head_grad,
    coarse_head_grad,
    fine_all,
    coarse_all,
    fine_acc,
    coarse_acc,
    unit_keep,
    inv_keep,
    rows_sib,
    consts,
    loss_acc,
    sib_out,
    sib_in,
    half_out,
    half_in,
    full_out,
    full_in,
    hop_out,
    hop_in,
    own_sum,
    dp_keep,
    dp_sib,
    part,
    part_out,
    part_in,
    quarter,
    quarter_out,
    quarter_in,
    column,
    whole,
    whole_sib,
    loss_parts,
    send_sem,
    recv_sem,
):
    rows, width = fine_rows.shape
    half = rows // 2
    wide = width // 2
    here = Place()
    copies = Copies(send_sem, recv_sem)
    upper, lower = pl.ds(0, half), pl.ds(half, half)

    def slot(step):
        return pl.ds((step % 4) * rows, rows)

    barrier = pltpu.get_barrier_semaphore()
    partners = [here.sibling]
    partners += [here.along(axis, step) for axis in "xyz" for step in (1, 2, 3)]
    for device in partners:
        pl.semaphore_signal(barrier, inc=1, device_id=device, device_id_type=MESH)

    consts[0] = 0.5 * jnp.exp(jnp.full((8, width), log_scale[0], F32))
    consts[1] = jnp.full((8, width), 0.5 * bias[0], F32)
    h, shift = consts[0, 0:1, :], consts[1, 0:1, :]

    def embed(which, rows_ref, head_ref):
        proj = dot(rows_ref[...], head_ref[...], NN)
        inv = lax.rsqrt(jnp.sum(proj * proj, axis=-1, keepdims=True) + EPS)
        unit = proj * inv
        unit_keep[which] = unit
        inv_keep[which] = inv
        return unit.astype(BF16)

    fine_all[0, slot(0)] = embed(0, fine_rows, fine_head)
    pl.semaphore_wait(barrier, len(partners))
    mine = (fine_all, 0, slot(0))
    copies.start("fz", mine, (fine_all, 2, slot(0)), here.other_hi)
    copies.start("fx+", mine, (fine_all, 0, slot(-1)), here.along("x", 1))
    copies.start("fx-", mine, (fine_all, 0, slot(1)), here.along("x", 3))
    copies.start("fs", mine, (fine_all, 1, slot(0)), here.sibling)

    coarse_all[0, slot(0)] = embed(1, coarse_rows, coarse_head)
    mine = (coarse_all, 0, slot(0))
    copies.start("cz", mine, (coarse_all, 1, slot(0)), here.other_lo)
    copies.start("cy+", mine, (coarse_all, 0, slot(-1)), here.along("y", 1))
    copies.start("cy-", mine, (coarse_all, 0, slot(1)), here.along("y", 3))
    copies.start("rf", (fine_rows,), (rows_sib, 0), here.sibling)
    copies.start("rc", (coarse_rows,), (rows_sib, 1), here.sibling)

    def pass_on(tag, axis, buf, at, sib_at):
        copies.wait(tag + "+")
        copies.start(tag + "++", (buf, at, pl.ds(3 * rows, half)), (buf, at, pl.ds(2 * rows, half)), here.along(axis, 1))
        if sib_at is not None:
            copies.start(tag + "+s", (buf, at, slot(-1)), (buf, sib_at, slot(-1)), here.sibling)
        copies.wait(tag + "-")
        copies.start(tag + "--", (buf, at, pl.ds(rows + half, half)), (buf, at, pl.ds(2 * rows + half, half)), here.along(axis, 3))
        if sib_at is not None:
            copies.start(tag + "-s", (buf, at, slot(1)), (buf, sib_at, slot(1)), here.sibling)

    def hand_over(tag, buf, at, sib_at):
        copies.wait(tag + "++", tag + "--")
        if sib_at is not None:
            copies.start(tag + "2s", (buf, at, slot(2)), (buf, sib_at, slot(2)), here.sibling)

    fine_acc[...] = jnp.zeros_like(fine_acc)
    coarse_acc[...] = jnp.zeros_like(coarse_acc)
    loss_acc[...] = jnp.zeros_like(loss_acc)

    fine_emb = fine_all[0, slot(0)].astype(F32)
    coarse_emb = coarse_all[0, slot(0)].astype(F32)
    arg = jnp.sum(fine_emb * coarse_emb, axis=-1, keepdims=True) * consts[0, 0:1, 0:1] + consts[1, 0:1, 0:1]
    tanh = jnp.tanh(arg)
    delta = (tanh - 1.0).astype(BF16).astype(F32) - (1.0 + tanh).astype(BF16).astype(F32)
    own_sum[0] = delta * coarse_emb
    own_sum[1] = delta * fine_emb
    diagonal = jnp.sum(2.0 * arg, axis=0, keepdims=True)

    pass_on("fx", "x", fine_all, 0, 1)
    pass_on("cy", "y", coarse_all, 0, None)
    copies.wait("fz")
    mine = (fine_all, 2, slot(0))
    copies.start("gx+", mine, (fine_all, 2, slot(-1)), here.along("x", 1))
    copies.start("gx-", mine, (fine_all, 2, slot(1)), here.along("x", 3))
    copies.start("gs", mine, (fine_all, 3, slot(0)), here.sibling)
    copies.wait("cz")
    mine = (coarse_all, 1, slot(0))
    copies.start("dy+", mine, (coarse_all, 1, slot(-1)), here.along("y", 1))
    copies.start("dy-", mine, (coarse_all, 1, slot(1)), here.along("y", 3))
    hand_over("fx", fine_all, 0, 1)
    hand_over("cy", coarse_all, 0, None)

    def tile(fg, cg):
        cols = coarse_all[cg]
        n = 256
        coefs = []
        for j in range(4 * rows // n):
            at = pl.ds(j * n, n)
            t = jnp.tanh(dot(fine_all[fg, at], cols, NT) * h + shift)
            coef = (1.0 + t).astype(BF16)
            rest = 1.0 - t
            eighth = n // 8
            p = [rest[i * eighth : (i + 1) * eighth] for i in range(8)]
            p = ((p[0] * p[1]) * (p[2] * p[3])) * ((p[4] * p[5]) * (p[6] * p[7]))
            p = jnp.log(p * (1.0 / 256.0))
            loss_acc[...] -= (p[0:8] + p[8:16]) + (p[16:24] + p[24:32])
            fine_acc[fg, at] += dot(coef, cols, NN)
            coefs.append(coef)
        coarse_acc[cg] += dot(jnp.concatenate(coefs, 0), fine_all[fg], TN)

    def to_sibling(k):
        sib_out[k] = fine_acc[2 * k + 1].astype(BF16)
        copies.start(f"sum_s{k}", (sib_out, k), (sib_in, k), here.sibling)

    def ring_start(tag, axis, r, acc, other):
        def total(step):
            value = acc[slot(step)]
            return value if other is None else value + other[slot(step)].astype(F32)

        half_out[r] = total(2).astype(BF16)
        copies.start(tag + "h+", (half_out, r, upper), (half_in, r, upper), here.along(axis, 1))
        copies.start(tag + "h-", (half_out, r, lower), (half_in, r, lower), here.along(axis, 3))
        if other is not None:
            for step in (0, 1, 3):
                acc[slot(step)] = total(step)

    def ring_middle(tag, axis, r, acc):
        copies.wait(tag + "h+")
        full_out[r, 0, upper] = (acc[pl.ds(rows, half)] + half_in[r, upper].astype(F32)).astype(BF16)
        full_out[r, 0, lower] = acc[pl.ds(rows + half, half)].astype(BF16)
        copies.start(tag + "f+", (full_out, r, 0), (full_in, r, 0), here.along(axis, 1))
        copies.wait(tag + "h-")
        full_out[r, 1, upper] = acc[pl.ds(3 * rows, half)].astype(BF16)
        full_out[r, 1, lower] = (acc[pl.ds(3 * rows + half, half)] + half_in[r, lower].astype(F32)).astype(BF16)
        copies.start(tag + "f-", (full_out, r, 1), (full_in, r, 1), here.along(axis, 3))

    def ring_end(tag, r, acc):
        copies.wait(tag + "f+", tag + "f-")
        return acc[slot(0)] + full_in[r, 0].astype(F32) + full_in[r, 1].astype(F32)

    def hop(tag, which, value, device):
        hop_out[which] = value.astype(BF16)
        copies.start(tag, (hop_out, which), (hop_in, which), device)

    def step(t, carry):
        @pl.when(t == 1)
        def _():
            copies.wait("fs", "fx+s", "fx-s", "fx2s")

        @pl.when(t == 2)
        def _():
            pass_on("gx", "x", fine_all, 2, 3)
            pass_on("dy", "y", coarse_all, 1, None)
            hand_over("gx", fine_all, 2, 3)

        @pl.when(t == 3)
        def _():
            copies.wait("gs", "gx+s", "gx-s", "gx2s")

        @pl.when(t == 4)
        def _():
            ring_start("c0", "y", 2, coarse_acc.at[0], None)
            hand_over("dy", coarse_all, 1, None)

        @pl.when(t == 5)
        def _():
            to_sibling(1)
            ring_middle("c0", "y", 2, coarse_acc.at[0])

        @pl.when(t == 6)
        def _():
            copies.wait("sum_s1")
            ring_start("f1", "x", 1, fine_acc.at[2], sib_in.at[1])
            own_sum[1] += ring_end("c0", 2, coarse_acc.at[0])

        @pl.when(t == 7)
        def _():
            to_sibling(0)
            ring_middle("f1", "x", 1, fine_acc.at[2])

        late = t // 4
        tile(t + late * (7 - 2 * t), late)
        return carry

    lax.fori_loop(0, 8, step, 0)

    copies.wait("sum_s0")
    ring_start("f0", "x", 0, fine_acc.at[0], sib_in.at[0])
    ring_start("c1", "y", 3, coarse_acc.at[1], None)
    hop("fhop", 0, ring_end("f1", 1, fine_acc.at[2]), here.other_hi)

    loss = loss_acc[:, 0:128]
    for i in range(1, width // 128):
        loss = loss + loss_acc[:, i * 128 : (i + 1) * 128]
    at_origin = (lax.broadcasted_iota(jnp.int32, (8, 128), 0) + lax.broadcasted_iota(jnp.int32, (8, 128), 1)) == 0
    loss = loss - jnp.where(at_origin, diagonal, 0.0)
    loss_parts[0, 0] = loss
    copies.start("loss_s", (loss_parts, 0, 0), (loss_parts, 0, 1), here.sibling)

    def loss_round(r, axis, place):
        if r == 1:
            copies.wait("loss_s")
            value = loss_parts[0, 0] + loss_parts[0, 1]
        else:
            copies.wait(*[f"loss{r - 1}{d}" for d in (1, 2, 3)])
            q = loss_parts
            value = (q[r - 1, 0] + q[r - 1, 1]) + (q[r - 1, 2] + q[r - 1, 3])
        if axis is None:
            return value
        loss_parts[r, place] = value
        for d in (1, 2, 3):
            copies.start(f"loss{r}{d}", (loss_parts, r, place), (loss_parts, r, place), here.along(axis, d))

    ring_middle("f0", "x", 0, fine_acc.at[0])
    ring_middle("c1", "y", 3, coarse_acc.at[1])
    loss_round(1, "x", here.x)

    def head_back(which, value):
        unit, inv = unit_keep[which], inv_keep[which]
        grad = value * h
        inner = jnp.sum(unit * grad, axis=-1, keepdims=True)
        dp = (inv * (grad - unit * inner)).astype(BF16)
        dp_keep[which, 0] = dp[:, 0:wide]
        dp_keep[which, 1] = dp[:, wide:]
        copies.start(f"dp{which}", (dp_keep, which, 1 - here.core), (dp_sib, which), here.sibling)

    def rows_grad(which, head_ref, out):
        head = head_ref[...]
        out[...] = dot(dp_keep[which, 0], head[:, 0:wide], NT) + dot(dp_keep[which, 1], head[:, wide:], NT)

    axes = {0: ("x", here.x, "y", here.y), 1: ("y", here.y, "x", here.x)}

    def head_part(which, rows_ref):
        first, at, _, _ = axes[which]
        copies.wait(f"dp{which}")
        value = dot(rows_ref[...], dp_keep[which, here.core], TN)
        value = value + dot(rows_sib[which], dp_sib[which], TN)
        for j in range(4):
            part[which, j] = value[j * rows : (j + 1) * rows]
            part_out[which, j] = value[j * rows : (j + 1) * rows].astype(BF16)
        for d in (1, 3, 2):
            copies.start(f"part{which}{d}", (part_out, which, (at + d) % 4), (part_in, which, d - 1), here.along(first, d))

    def head_quarter(which):
        _, at, second, place = axes[which]
        copies.wait(*[f"part{which}{d}" for d in (1, 2, 3)])
        value = part[which, at]
        for d in range(3):
            value = value + part_in[which, d].astype(F32)
        n = rows // 4
        for j in range(4):
            quarter[which, j] = value[j * n : (j + 1) * n]
            quarter_out[which, j] = value[j * n : (j + 1) * n].astype(BF16)
        for d in (1, 3, 2):
            copies.start(f"quarter{which}{d}", (quarter_out, which, (place + d) % 4), (quarter_in, which, d - 1), here.along(second, d))

    def head_column(which):
        _, _, _, place = axes[which]
        copies.wait(*[f"quarter{which}{d}" for d in (1, 2, 3)])
        value = quarter[which, place]
        for d in range(3):
            value = value + quarter_in[which, d].astype(F32)
        column[which, here.z] = value.astype(BF16)
        mine = (column, which, here.z)
        for d in (1, 3, 2):
            copies.start(f"column{which}{d}", mine, mine, here.along("z", d))

    def head_total(which):
        _, at, second, place = axes[which]
        copies.wait(*[f"column{which}{d}" for d in (1, 2, 3)])
        value = column[which, 0].astype(F32)
        for z in range(1, 4):
            value = value + column[which, z].astype(F32)
        whole[which, at, place] = value.astype(BF16)
        mine = (whole, which, at, place)
        for d in (1, 3, 2):
            copies.start(f"back{which}{d}", mine, mine, here.along(second, d))

    def head_spread(which):
        first, at, _, _ = axes[which]
        copies.wait(*[f"back{which}{d}" for d in (1, 2, 3)])
        mine = (whole, which, at)
        for d in (1, 3, 2):
            copies.start(f"spread{which}{d}", mine, mine, here.along(first, d))

    def head_share(which, out):
        copies.wait(*[f"spread{which}{d}" for d in (1, 2, 3)])
        copies.start(f"share{which}", (whole, which), (whole_sib, which), here.sibling)
        cols = pl.ds(pl.multiple_of(here.core * wide, 128), wide)
        n = rows // 4
        for i in range(4):
            for j in range(4):
                out[pl.ds(i * rows + j * n, n), cols] = whole[which, i, j].astype(F32)

    def head_write(which, out):
        copies.wait(f"share{which}")
        cols = pl.ds(pl.multiple_of((1 - here.core) * wide, 128), wide)
        n = rows // 4
        for i in range(4):
            for j in range(4):
                out[pl.ds(i * rows + j * n, n), cols] = whole_sib[which, i, j].astype(F32)

    value = ring_end("f0", 0, fine_acc.at[0]) + own_sum[0]
    copies.wait("fhop")
    head_back(0, value + hop_in[0].astype(F32))
    hop("chop", 1, ring_end("c1", 3, coarse_acc.at[1]), here.other_lo)
    copies.wait("rf", "rc")
    head_part(0, fine_rows)
    loss_round(2, "y", here.y)
    rows_grad(0, fine_head, fine_grad)
    copies.wait("chop")
    head_back(1, own_sum[1] + hop_in[1].astype(F32))
    head_part(1, coarse_rows)
    rows_grad(1, coarse_head, coarse_grad)
    loss_round(3, "z", here.z)
    head_quarter(0)
    head_quarter(1)
    head_column(0)
    head_column(1)
    head_total(0)
    head_total(1)
    head_spread(0)
    head_spread(1)
    total = loss_round(4, None, None)
    pairs = float(rows * 128) ** 2
    loss_out[0] = jnp.sum(total) * (1.0 / pairs)
    head_share(0, fine_head_grad)
    head_share(1, coarse_head_grad)
    head_write(0, fine_head_grad)
    head_write(1, coarse_head_grad)
    copies.finish()


def shards(fine_rows, coarse_rows, fine_head, coarse_head, log_scale, bias):
    rows, width = fine_rows.shape
    wide, n = width // 2, rows // 4
    vmem = pl.BlockSpec(memory_space=pltpu.VMEM)
    smem = pl.BlockSpec(memory_space=pltpu.SMEM)
    scratch = [
        VMEM((4, 4 * rows, width), BF16),
        VMEM((2, 4 * rows, width), BF16),
        VMEM((4, 4 * rows, width), F32),
        VMEM((2, 4 * rows, width), F32),
        VMEM((2, rows, width), F32),
        VMEM((2, rows, 1), F32),
        VMEM((2, rows, width), BF16),
        VMEM((2, 8, width), F32),
        VMEM((8, width), F32),
        VMEM((2, 4 * rows, width), BF16),
        VMEM((2, 4 * rows, width), BF16),
        VMEM((4, rows, width), BF16),
        VMEM((4, rows, width), BF16),
        VMEM((4, 2, rows, width), BF16),
        VMEM((4, 2, rows, width), BF16),
        VMEM((2, rows, width), BF16),
        VMEM((2, rows, width), BF16),
        VMEM((2, rows, width), F32),
        VMEM((2, 2, rows, wide), BF16),
        VMEM((2, rows, wide), BF16),
        VMEM((2, 4, rows, wide), F32),
        VMEM((2, 4, rows, wide), BF16),
        VMEM((2, 3, rows, wide), BF16),
        VMEM((2, 4, n, wide), F32),
        VMEM((2, 4, n, wide), BF16),
        VMEM((2, 3, n, wide), BF16),
        VMEM((2, 4, n, wide), BF16),
        VMEM((2, 4, 4, n, wide), BF16),
        VMEM((2, 4, 4, n, wide), BF16),
        VMEM((4, 4, 8, 128), F32),
        pltpu.SemaphoreType.DMA((N_COPIES,)),
        pltpu.SemaphoreType.DMA((N_COPIES,)),
    ]
    tokens = rows * lax.axis_size("grp") * lax.axis_size("mem")
    pair_flops = 6 * (16 * rows) * (8 * rows) * width
    return pl.pallas_call(
        kernel,
        out_shape=(
            jax.ShapeDtypeStruct((1,), F32),
            jax.ShapeDtypeStruct((rows, width), F32),
            jax.ShapeDtypeStruct((rows, width), F32),
            jax.ShapeDtypeStruct((width, width), F32),
            jax.ShapeDtypeStruct((width, width), F32),
        ),
        in_specs=[vmem, vmem, vmem, vmem, smem, smem],
        out_specs=(smem, vmem, vmem, vmem, vmem),
        scratch_shapes=scratch,
        cost_estimate=pl.CostEstimate(flops=pair_flops, bytes_accessed=tokens * width, transcendentals=0),
        compiler_params=pltpu.CompilerParams(collective_id=0, has_side_effects=True, vmem_limit_bytes=58 * 2**20),
    )(fine_rows, coarse_rows, fine_head, coarse_head, log_scale, bias)


def solution(mesh):
    placed = (P(("grp", "mem"), None), P(("grp", "mem"), None), P(), P(), P(), P())
    return jax.shard_map(
        shards,
        mesh=mesh,
        in_specs=placed,
        out_specs=(P(), P(("grp", "mem"), None), P(("grp", "mem"), None), P(), P()),
        check_vma=False,
    )
```

time: 459 us -> 131 us (0.29)
  waiting for transfers between devices: 300 us -> 0 us
  Pallas kernels: 0 us -> 119 us
  blocking collectives: 65.5 us -> 0 us
  matrix products: 58.7 us -> 0 us
  between operations: 17 us -> 3.85 us
  other arithmetic: 6.34 us -> 0 us
    pallas_call x0 -> x1, Pallas kernels: none -> 119 us  [shards(): pl.pallas_call(kernel, out_shape=(jax.ShapeDtypeStruct((1,), F32), jax.Sh...]
    reduce_scatter x2 -> x0, waiting for transfers between devices: 110 us -> none  [the longest x1 85.7 us: shards(): lax.psum_scatter(acc_rows.astype(jnp.bfloat16), 'mem', scatter_dimension=...]
    all_gather x2 -> x0, waiting for transfers between devices: 102 us -> none  [the longest x1 65.5 us: shards(): rows_block = lax.all_gather(fine_emb, 'mem', axis=0, tiled=True)]
    psum x1 -> x0, waiting for transfers between devices: 88.5 us -> none  [shards(): lax.psum((fine_part, coarse_part, total), ('grp', 'mem'))]
    psum x1 -> x0, blocking collectives: 65.5 us -> none  [shards(): lax.psum((fine_part, coarse_part, total), ('grp', 'mem'))]
    dot_general x9 -> x0, matrix products: 58.7 us -> none  [the longest x1 27.4 us: pair_tile(): lax.dot_general(rows_part, cols_part, (((1,), (1,)), ((), ())), preferred...]
    unnamed x16 -> x8, local copies, waits for them, and re-layouts: 10 us -> 7.76 us
  transfers between devices with their start and end apart: 5 -> 0, of which waited for: 5 -> 0; matrix products, arithmetic and copies ran while one was open for 5% -> 0% of each run, Pallas kernels for 0% -> 0%
where the time goes in v1:
time: 131 us
  Pallas kernels  119 us (91%)
  local copies, waits for them, and re-layouts  7.76 us (6%)
  between operations  3.85 us (3%)
    pallas_call x1, Pallas kernels, shards(): pl.pallas_call(kernel, out_shape=(jax.ShapeDtypeStruct((1,), F32), jax.Sh...  119 us
    unnamed x8, local copies, waits for them, and re-layouts  7.76 us

profile of v1, /device:TPU:1, one launch (start us, length us, event | category | flops | bytes accessed | tf_op | source)
XLA Modules:
  0.0 130.5 jit_solution(15164220453797791881)
XLA Ops:
  1.9 118.9 %shard_map.101 = (f32[1]{0:T(128)}, f32[192,768]{1,0:T(8,128)}, f32[192,768]{1,0:T(8,128)}, f32[768,768]{1,0:T(8,128)}, f32[768,768]{1,0:T(8,128)}) custom-call(bf16[192,768]{1,0:T(8,128)(2,1)} %fine_rows.1, bf16[192,768]{1,0:T(8,128)(2,1)} %coarse_rows.1, bf16[768,768]{1,0:T(8,128)(2,1)} %fine_head.1, bf16[768,768]{1,0:T(8,128)(2,1)} %coarse_head.1, ...), custom_call_target="tpu_custom_call" | custom-call | flops 21743271936 | bytes 18874368 | tf_op jit(solution)/shard_map/pallas_call | solution.py:498
  120.8 0.0 copy-start.1
  121.6 1.9 %copy.19 = f32[192,768]{1,0:T(8,128)} copy(f32[192,768]{1,0:T(8,128)} %get-tuple-element.11) | data formatting | bytes 1179648
  123.5 1.9 %copy.20 = f32[192,768]{1,0:T(8,128)} copy(f32[192,768]{1,0:T(8,128)} %get-tuple-element.12) | data formatting | bytes 1179648
  125.5 0.0 copy-done.1
  125.5 0.0 copy-start
  125.5 1.4 %copy.21 = f32[768,768]{1,0:T(8,128)} copy(f32[768,768]{1,0:T(8,128)S(1)} %copy-done.1) | data formatting | bytes 4718592
  126.9 1.1 copy-done
  128.0 1.4 %copy.22 = f32[768,768]{1,0:T(8,128)} copy(f32[768,768]{1,0:T(8,128)S(1)} %copy-done) | data formatting | bytes 4718592
Async XLA Ops:
  120.8 4.6 %copy-start.1 = (f32[768,768]{1,0:T(8,128)S(1)}, f32[768,768]{1,0:T(8,128)}, u32[]{:S(2)}) copy-start(f32[768,768]{1,0:T(8,128)} %get-tuple-element.13) | copy-start | bytes 7077892
  125.5 2.5 %copy-start = (f32[768,768]{1,0:T(8,128)S(1)}, f32[768,768]{1,0:T(8,128)}, u32[]{:S(2)}) copy-start(f32[768,768]{1,0:T(8,128)} %get-tuple-element.14) | copy-start | bytes 7077892

commit v2 on v1

v2 whole, which is shorter than its diff:
```python
import jax
import jax.numpy as jnp
from jax import lax
from jax.experimental import pallas as pl
from jax.experimental.pallas import tpu as pltpu
from jax.sharding import PartitionSpec as P

MESH = pl.DeviceIdType.MESH
EPS = 1e-06
F32 = jnp.float32
BF16 = jnp.bfloat16
VMEM = pltpu.VMEM


def dot(a, b, dims):
    return lax.dot_general(a, b, (dims, ((), ())), preferred_element_type=F32)


NN = ((1,), (0,))
NT = ((1,), (1,))
TN = ((0,), (0,))


class Place:
    def __init__(self):
        grp, mem = lax.axis_index("grp"), lax.axis_index("mem")
        self.core = mem % 2
        self.x, self.y = (mem // 2) % 4, grp % 4
        self.z = (mem // 8) * 2 + grp // 4
        self.steps = {("x", d): self.at(dx=d) for d in (1, 2, 3)}
        self.steps |= {("y", d): self.at(dy=d) for d in (1, 2, 3)}
        self.steps |= {("z", d): self.at(z=(self.z + d) % 4) for d in (1, 2, 3)}
        self.sibling = self.at(core=1 - self.core)
        self.other_hi = self.steps["z", 2]
        self.other_lo = self.at(z=self.z + 1 - 2 * (self.z % 2))

    def at(self, dx=0, dy=0, z=None, core=None):
        x, y = (self.x + dx) % 4, (self.y + dy) % 4
        z = self.z if z is None else z
        core = self.core if core is None else core
        return ((z % 2) * 4 + y, (z // 2) * 8 + x * 2 + core)

    def along(self, axis, step):
        return self.steps[axis, step]


def view(ref, *index):
    return ref.at[index] if index else ref


class Copies:
    def __init__(self, send_sem, recv_sem):
        self.send_sem, self.recv_sem = send_sem, recv_sem
        self.made = {}

    def start(self, name, src, dst, device):
        index = len(self.made)
        assert name not in self.made and index < N_COPIES

        def make():
            return pltpu.make_async_remote_copy(
                src_ref=view(*src),
                dst_ref=view(*dst),
                send_sem=self.send_sem.at[index],
                recv_sem=self.recv_sem.at[index],
                device_id=device,
                device_id_type=MESH,
            )

        self.made[name] = make
        make().start()

    def wait(self, *names):
        for name in names:
            self.made[name]().wait_recv()

    def finish(self):
        for make in self.made.values():
            make().wait_send()


N_COPIES = 128
ORDERS = (("x", "y", "z"), ("y", "z", "x"), ("z", "x", "y"))


def kernel(
    fine_rows,
    coarse_rows,
    fine_head,
    coarse_head,
    log_scale,
    bias,
    loss_out,
    fine_grad_out,
    coarse_grad_out,
    heads_out,
    fine_all,
    coarse_all,
    fine_acc,
    coarse_acc,
    unit_keep,
    inv_keep,
    rows_keep,
    consts,
    loss_acc,
    sib_out,
    sib_in,
    half_out,
    half_in,
    full_out,
    full_in,
    hop_out,
    hop_in,
    own_sum,
    dp_keep,
    grad_keep,
    part_out,
    part_in,
    quarter_out,
    quarter_in,
    column,
    heads,
    loss_parts,
    send_sem,
    recv_sem,
    local_sem,
):
    rows, width = fine_rows.shape
    half = rows // 2
    wide = width // 2
    here = Place()
    copies = Copies(send_sem, recv_sem)
    upper, lower = pl.ds(0, half), pl.ds(half, half)

    def slot(step):
        return pl.ds((step % 4) * rows, rows)

    def slot_half(step, which):
        return pl.ds((step % 4) * rows + which * half, half)

    barrier = pltpu.get_barrier_semaphore()
    partners = [here.sibling]
    partners += [here.along(axis, step) for axis in "xyz" for step in (1, 2, 3)]
    for device in partners:
        pl.semaphore_signal(barrier, inc=1, device_id=device, device_id_type=MESH)

    consts[0] = 0.5 * jnp.exp(jnp.full((8, width), log_scale[0], F32))
    consts[1] = jnp.full((8, width), 0.5 * bias[0], F32)
    h, shift = consts[0, 0:1, :], consts[1, 0:1, :]
    inputs = (fine_rows, coarse_rows)

    def embed(which, far, part, head_ref):
        at = pl.ds(part * half, half)
        proj = dot(rows_keep[which, pl.ds(far * rows + part * half, half)], head_ref[...], NN)
        inv = lax.rsqrt(jnp.sum(proj * proj, axis=-1, keepdims=True) + EPS)
        unit = proj * inv
        unit_keep[which, far, at] = unit
        inv_keep[which, far, at] = inv
        return unit.astype(BF16)

    for which in (0, 1):
        rows_keep[which, pl.ds(0, rows)] = inputs[which][...]
    pl.semaphore_wait(barrier, len(partners))
    far_device = (here.other_hi, here.other_lo)
    for part in (0, 1):
        for which in (0, 1):
            copies.start(
                f"z{which}{part}",
                (rows_keep, which, pl.ds(part * half, half)),
                (rows_keep, which, pl.ds(rows + part * half, half)),
                far_device[which],
            )

    def send_both(tag, axis, buf, at, order_plus, order_minus):
        for p in order_plus:
            copies.start(f"{tag}+{p}", (buf, at, slot_half(0, p)), (buf, at, slot_half(-1, p)), here.along(axis, 1))
        for p in order_minus:
            copies.start(f"{tag}-{p}", (buf, at, slot_half(0, p)), (buf, at, slot_half(1, p)), here.along(axis, 3))

    def pass_plus(tag, axis, buf, at):
        copies.wait(tag + "+0")
        copies.start(tag + "++", (buf, at, slot_half(-1, 0)), (buf, at, slot_half(2, 0)), here.along(axis, 1))

    def pass_minus(tag, axis, buf, at):
        copies.wait(tag + "-1")
        copies.start(tag + "--", (buf, at, slot_half(1, 1)), (buf, at, slot_half(2, 1)), here.along(axis, 3))

    def sib_near(tag, at):
        copies.wait(tag + "+1")
        copies.start(tag + "+s", (fine_all, at, slot(-1)), (fine_all, at + 1, slot(-1)), here.sibling)
        copies.wait(tag + "-0")
        copies.start(tag + "-s", (fine_all, at, slot(1)), (fine_all, at + 1, slot(1)), here.sibling)

    def sib_far(tag, at):
        copies.wait(tag + "++", tag + "--")
        copies.start(tag + "2s", (fine_all, at, slot(2)), (fine_all, at + 1, slot(2)), here.sibling)

    for p in (0, 1):
        fine_all[0, slot_half(0, p)] = embed(0, 0, p, fine_head)
    send_both("fx", "x", fine_all, 0, (0, 1), (1, 0))
    copies.start("fs", (fine_all, 0, slot(0)), (fine_all, 1, slot(0)), here.sibling)
    for p in (0, 1):
        coarse_all[0, slot_half(0, p)] = embed(1, 0, p, coarse_head)
    send_both("cy", "y", coarse_all, 0, (0, 1), (1, 0))

    coarse_acc[...] = jnp.zeros_like(coarse_acc)
    loss_acc[...] = jnp.zeros_like(loss_acc)

    fine_emb = fine_all[0, slot(0)].astype(F32)
    coarse_emb = coarse_all[0, slot(0)].astype(F32)
    arg = jnp.sum(fine_emb * coarse_emb, axis=-1, keepdims=True) * consts[0, 0:1, 0:1] + consts[1, 0:1, 0:1]
    tanh = jnp.tanh(arg)
    delta = (tanh - 1.0).astype(BF16).astype(F32) - (1.0 + tanh).astype(BF16).astype(F32)
    own_sum[0] = delta * coarse_emb
    own_sum[1] = delta * fine_emb
    diagonal = jnp.sum(2.0 * arg, axis=0, keepdims=True)

    pass_plus("fx", "x", fine_all, 0)
    pass_plus("cy", "y", coarse_all, 0)
    pass_minus("fx", "x", fine_all, 0)
    pass_minus("cy", "y", coarse_all, 0)
    for p in (0, 1):
        copies.wait(f"z0{p}")
        fine_all[2, slot_half(0, p)] = embed(0, 1, p, fine_head)
        for sign, step in (("+", 1), ("-", 3)):
            copies.start(f"gx{sign}{p}", (fine_all, 2, slot_half(0, p)), (fine_all, 2, slot_half(-step, p)), here.along("x", step))
        copies.wait(f"z1{p}")
        coarse_all[1, slot_half(0, p)] = embed(1, 1, p, coarse_head)
        for sign, step in (("+", 1), ("-", 3)):
            copies.start(f"dy{sign}{p}", (coarse_all, 1, slot_half(0, p)), (coarse_all, 1, slot_half(-step, p)), here.along("y", step))
    sib_near("fx", 0)
    copies.start("gs", (fine_all, 2, slot(0)), (fine_all, 3, slot(0)), here.sibling)
    for which in (0, 1):
        copies.start(f"rows{which}", (rows_keep, which, pl.ds(0, 2 * rows)), (rows_keep, which, pl.ds(2 * rows, 2 * rows)), here.sibling)
    fine_acc[...] = jnp.zeros_like(fine_acc)
    copies.wait("cy+1", "cy-0", "cy++", "cy--")
    sib_far("fx", 0)

    def tile(fg, cg):
        cols = coarse_all[cg]
        n = 256
        coefs = []
        for j in range(4 * rows // n):
            at = pl.ds(j * n, n)
            t = jnp.tanh(dot(fine_all[fg, at], cols, NT) * h + shift)
            coef = (1.0 + t).astype(BF16)
            rest = 1.0 - t
            eighth = n // 8
            p = [rest[i * eighth : (i + 1) * eighth] for i in range(8)]
            p = ((p[0] * p[1]) * (p[2] * p[3])) * ((p[4] * p[5]) * (p[6] * p[7]))
            p = jnp.log(p * (1.0 / 256.0))
            loss_acc[...] -= (p[0:8] + p[8:16]) + (p[16:24] + p[24:32])
            fine_acc[fg, at] += dot(coef, cols, NN)
            coefs.append(coef)
        coarse_acc[cg] += dot(jnp.concatenate(coefs, 0), fine_all[fg], TN)

    def to_sibling(k):
        sib_out[k] = fine_acc[2 * k + 1].astype(BF16)
        copies.start(f"sum_s{k}", (sib_out, k), (sib_in, k), here.sibling)

    def ring_start(tag, axis, r, acc, a, other):
        def total(step, p):
            value = acc[a, slot_half(step, p)]
            return value if other is None else value + sib_in[other, slot_half(step, p)].astype(F32)

        plus, minus = here.along(axis, 1), here.along(axis, 3)
        half_out[r, upper] = total(2, 0).astype(BF16)
        copies.start(tag + "h+", (half_out, r, upper), (half_in, r, upper), plus)
        half_out[r, lower] = total(2, 1).astype(BF16)
        copies.start(tag + "h-", (half_out, r, lower), (half_in, r, lower), minus)
        full_out[r, 0, lower] = total(1, 1).astype(BF16)
        copies.start(tag + "f+1", (full_out, r, 0, lower), (full_in, r, 0, lower), plus)
        full_out[r, 1, upper] = total(3, 0).astype(BF16)
        copies.start(tag + "f-0", (full_out, r, 1, upper), (full_in, r, 1, upper), minus)
        if other is not None:
            for step, p in ((1, 0), (3, 1), (0, 0), (0, 1)):
                acc[a, slot_half(step, p)] = total(step, p)

    def ring_middle(tag, axis, r, acc, a):
        copies.wait(tag + "h+")
        full_out[r, 0, upper] = (acc[a, slot_half(1, 0)] + half_in[r, upper].astype(F32)).astype(BF16)
        copies.start(tag + "f+0", (full_out, r, 0, upper), (full_in, r, 0, upper), here.along(axis, 1))
        copies.wait(tag + "h-")
        full_out[r, 1, lower] = (acc[a, slot_half(3, 1)] + half_in[r, lower].astype(F32)).astype(BF16)
        copies.start(tag + "f-1", (full_out, r, 1, lower), (full_in, r, 1, lower), here.along(axis, 3))

    def ring_end(tag, r, acc, a):
        copies.wait(tag + "f+0", tag + "f+1", tag + "f-0", tag + "f-1")
        return acc[a, slot(0)] + full_in[r, 0].astype(F32) + full_in[r, 1].astype(F32)

    def hop(which, value):
        hop_out[which] = value.astype(BF16)
        copies.start(f"hop{which}", (hop_out, which), (hop_in, which), far_device[which])

    def step(t, carry):
        @pl.when(t == 1)
        def _():
            pass_plus("gx", "x", fine_all, 2)
            pass_plus("dy", "y", coarse_all, 1)
            copies.wait("fs", "fx+s", "fx-s", "fx2s")

        @pl.when(t == 2)
        def _():
            pass_minus("gx", "x", fine_all, 2)
            pass_minus("dy", "y", coarse_all, 1)
            sib_near("gx", 2)
            sib_far("gx", 2)

        @pl.when(t == 3)
        def _():
            copies.wait("gs", "gx+s", "gx-s", "gx2s")

        @pl.when(t == 4)
        def _():
            ring_start("c0", "y", 2, coarse_acc, 0, None)
            copies.wait("dy+1", "dy-0", "dy++", "dy--")

        @pl.when(t == 5)
        def _():
            to_sibling(1)
            ring_middle("c0", "y", 2, coarse_acc, 0)

        @pl.when(t == 6)
        def _():
            copies.wait("sum_s1")
            ring_start("f1", "x", 1, fine_acc, 2, 1)
            own_sum[1] += ring_end("c0", 2, coarse_acc, 0)

        @pl.when(t == 7)
        def _():
            to_sibling(0)
            ring_middle("f1", "x", 1, fine_acc, 2)

        late = t // 4
        tile(t + late * (7 - 2 * t), late)
        return carry

    lax.fori_loop(0, 8, step, 0)

    def back(which, far, value):
        unit, inv = unit_keep[which, far], inv_keep[which, far]
        grad = value * h
        inner = jnp.sum(unit * grad, axis=-1, keepdims=True)
        return (inv * (grad - unit * inner)).astype(BF16)

    def keep(which, far, value):
        dp = back(which, far, value)
        for i in (0, 1):
            dp_keep[which, i, pl.ds(far * rows, rows)] = dp[:, i * wide : (i + 1) * wide]

    def dp_to_sibling(which):
        other = 1 - here.core
        copies.start(f"dp{which}", (dp_keep, which, other, pl.ds(0, 2 * rows)), (dp_keep, which, other, pl.ds(2 * rows, 2 * rows)), here.sibling)

    def grad_to_out(which, value, head_ref, out):
        grad_keep[which] = dot(back(which, 0, value), head_ref[...], NT)
        return pltpu.make_async_copy(grad_keep.at[which], out, local_sem.at[which])

    copies.wait("sum_s0")
    ring_start("f0", "x", 0, fine_acc, 0, 0)
    ring_start("c1", "y", 3, coarse_acc, 1, None)
    value = ring_end("f1", 1, fine_acc, 2)
    hop(0, value)
    keep(0, 1, value)

    loss = loss_acc[:, 0:128]
    for i in range(1, width // 128):
        loss = loss + loss_acc[:, i * 128 : (i + 1) * 128]
    at_origin = (lax.broadcasted_iota(jnp.int32, (8, 128), 0) + lax.broadcasted_iota(jnp.int32, (8, 128), 1)) == 0
    loss = loss - jnp.where(at_origin, diagonal, 0.0)
    loss_parts[0, 0] = loss
    copies.start("loss_s", (loss_parts, 0, 0), (loss_parts, 0, 1), here.sibling)

    def loss_round(r, axis, place):
        if r == 1:
            copies.wait("loss_s")
            value = loss_parts[0, 0] + loss_parts[0, 1]
        else:
            copies.wait(*[f"loss{r - 1}{d}" for d in (1, 2, 3)])
            q = loss_parts
            value = (q[r - 1, 0] + q[r - 1, 1]) + (q[r - 1, 2] + q[r - 1, 3])
        if axis is None:
            return value
        loss_parts[r, place] = value
        for d in (1, 2, 3):
            copies.start(f"loss{r}{d}", (loss_parts, r, place), (loss_parts, r, place), here.along(axis, d))

    ring_middle("f0", "x", 0, fine_acc, 0)
    ring_middle("c1", "y", 3, coarse_acc, 1)
    loss_round(1, "x", here.x)
    keep(1, 0, own_sum[1])
    value = ring_end("f0", 0, fine_acc, 0) + own_sum[0]
    own_sum[0] = value
    keep(0, 0, value)
    dp_to_sibling(0)
    value = ring_end("c1", 3, coarse_acc, 1)
    keep(1, 1, value)
    dp_to_sibling(1)
    hop(1, value)
    loss_round(2, "y", here.y)

    place = {"x": here.x, "y": here.y, "z": here.z}
    core = here.core
    n = rows // 4
    for which in (0, 1):
        copies.wait(f"rows{which}", f"dp{which}")
        value = dot(rows_keep[which], dp_keep[which, core], TN)
        for q in range(3):
            for j in range(4):
                part_out[q, j, which] = value[j * rows : (j + 1) * rows, q * 128 : (q + 1) * 128].astype(BF16)
    for d in (1, 3, 2):
        for q, (first, _, _) in enumerate(ORDERS):
            copies.start(f"part{q}{d}", (part_out, q, (place[first] + d) % 4), (part_in, q, d - 1), here.along(first, d))

    copies.wait("hop0")
    fine_copy = grad_to_out(0, own_sum[0] + hop_in[0].astype(F32), fine_head, fine_grad_out)
    fine_copy.start()
    copies.wait("hop1")
    coarse_copy = grad_to_out(1, own_sum[1] + hop_in[1].astype(F32), coarse_head, coarse_grad_out)
    coarse_copy.start()

    for q, (first, second, _) in enumerate(ORDERS):
        copies.wait(*[f"part{q}{d}" for d in (1, 2, 3)])
        value = part_out[q, place[first]].astype(F32)
        for d in range(3):
            value = value + part_in[q, d].astype(F32)
        for j in range(4):
            quarter_out[q, j] = value[:, j * n : (j + 1) * n].astype(BF16)
        for d in (1, 3, 2):
            copies.start(f"quarter{q}{d}", (quarter_out, q, (place[second] + d) % 4), (quarter_in, q, d - 1), here.along(second, d))
    loss_round(3, "z", here.z)
    for q, (_, second, third) in enumerate(ORDERS):
        copies.wait(*[f"quarter{q}{d}" for d in (1, 2, 3)])
        value = quarter_out[q, place[second]].astype(F32)
        for d in range(3):
            value = value + quarter_in[q, d].astype(F32)
        column[q, place[third]] = value.astype(BF16)
        mine = (column, q, place[third])
        for d in (1, 3, 2):
            copies.start(f"column{q}{d}", mine, mine, here.along(third, d))
    for q, (first, second, third) in enumerate(ORDERS):
        copies.wait(*[f"column{q}{d}" for d in (1, 2, 3)])
        value = column[q, 0].astype(F32)
        for i in range(1, 4):
            value = value + column[q, i].astype(F32)
        heads[core, q, place[first], place[second]] = value.astype(BF16)
        mine = (heads, core, q, place[first], place[second])
        for d in (1, 3, 2):
            copies.start(f"back{q}{d}", mine, mine, here.along(second, d))
    loss_out[...] = loss_round(4, None, None)
    for q, (first, second, _) in enumerate(ORDERS):
        copies.wait(*[f"back{q}{d}" for d in (1, 2, 3)])
        mine = (heads, core, q, place[first])
        for d in (1, 3, 2):
            copies.start(f"spread{q}{d}", mine, mine, here.along(first, d))
    for q in range(3):
        copies.wait(*[f"spread{q}{d}" for d in (1, 2, 3)])
        copies.start(f"share{q}", (heads, core, q), (heads, core, q), here.sibling)
    mine_copy = pltpu.make_async_copy(heads.at[core], heads_out.at[core], local_sem.at[2])
    mine_copy.start()
    copies.wait("share0", "share1", "share2")
    other_copy = pltpu.make_async_copy(heads.at[1 - core], heads_out.at[1 - core], local_sem.at[3])
    other_copy.start()
    copies.finish()
    fine_copy.wait()
    coarse_copy.wait()
    mine_copy.wait()
    other_copy.wait()


def place_results(pairs, loss_in, fine_in, coarse_in, heads, loss, fine_grad, coarse_grad, fine_head_grad, coarse_head_grad):
    loss[0] = jnp.sum(loss_in[...]) * (1.0 / pairs)
    fine_grad[...] = fine_in[...]
    coarse_grad[...] = coarse_in[...]
    halves, parts, _, pieces, _, n, lanes = heads.shape
    for side in range(halves):
        for q in range(parts):
            cols = pl.ds((side * parts + q) * lanes, lanes)
            for j in range(pieces):
                at = pl.ds(j * n, n)
                fine_head_grad[at, cols] = heads[side, q, 0, j, 0].astype(F32)
                coarse_head_grad[at, cols] = heads[side, q, 0, j, 1].astype(F32)


def shards(fine_rows, coarse_rows, fine_head, coarse_head, log_scale, bias):
    rows, width = fine_rows.shape
    wide, n = width // 2, rows // 4
    vmem = pl.BlockSpec(memory_space=pltpu.VMEM)
    smem = pl.BlockSpec(memory_space=pltpu.SMEM)
    anywhere = pl.BlockSpec(memory_space=pl.ANY)
    scratch = [
        VMEM((4, 4 * rows, width), BF16),
        VMEM((2, 4 * rows, width), BF16),
        VMEM((4, 4 * rows, width), F32),
        VMEM((2, 4 * rows, width), F32),
        VMEM((2, 2, rows, width), F32),
        VMEM((2, 2, rows, 1), F32),
        VMEM((2, 4 * rows, width), BF16),
        VMEM((2, 8, width), F32),
        VMEM((8, width), F32),
        VMEM((2, 4 * rows, width), BF16),
        VMEM((2, 4 * rows, width), BF16),
        VMEM((4, rows, width), BF16),
        VMEM((4, rows, width), BF16),
        VMEM((4, 2, rows, width), BF16),
        VMEM((4, 2, rows, width), BF16),
        VMEM((2, rows, width), BF16),
        VMEM((2, rows, width), BF16),
        VMEM((2, rows, width), F32),
        VMEM((2, 2, 4 * rows, wide), BF16),
        VMEM((2, rows, width), F32),
        VMEM((3, 4, 2, rows, 128), BF16),
        VMEM((3, 3, 2, rows, 128), BF16),
        VMEM((3, 4, 2, n, 128), BF16),
        VMEM((3, 3, 2, n, 128), BF16),
        VMEM((3, 4, 2, n, 128), BF16),
        VMEM((2, 3, 4, 4, 2, n, 128), BF16),
        VMEM((4, 4, 8, 128), F32),
        pltpu.SemaphoreType.DMA((N_COPIES,)),
        pltpu.SemaphoreType.DMA((N_COPIES,)),
        pltpu.SemaphoreType.DMA((4,)),
    ]
    tokens = rows * lax.axis_size("grp") * lax.axis_size("mem")
    pair_flops = 6 * (16 * rows) * (8 * rows) * width
    grad = jax.ShapeDtypeStruct((rows, width), F32)
    head = jax.ShapeDtypeStruct((width, width), F32)
    loss, fine_grad, coarse_grad, heads = pl.pallas_call(
        kernel,
        out_shape=(
            jax.ShapeDtypeStruct((8, 128), F32),
            grad,
            grad,
            jax.ShapeDtypeStruct((2, 3, 4, 4, 2, n, 128), BF16),
        ),
        in_specs=[vmem, vmem, vmem, vmem, smem, smem],
        out_specs=(vmem, anywhere, anywhere, anywhere),
        scratch_shapes=scratch,
        cost_estimate=pl.CostEstimate(flops=pair_flops, bytes_accessed=tokens * width, transcendentals=0),
        compiler_params=pltpu.CompilerParams(collective_id=0, has_side_effects=True, vmem_limit_bytes=60 * 2**20),
    )(fine_rows, coarse_rows, fine_head, coarse_head, log_scale, bias)

    def place(*refs):
        place_results(float(tokens) ** 2, *refs)

    by_rows = pl.BlockSpec((rows, width), lambda i: (i, 0))
    by_quarters = pl.BlockSpec((n, width), lambda i: (i, 0))
    return pl.pallas_call(
        place,
        grid=(4,),
        out_shape=(jax.ShapeDtypeStruct((1,), F32), grad, grad, head, head),
        in_specs=[
            pl.BlockSpec((8, 128), lambda i: (0, 0)),
            by_quarters,
            by_quarters,
            pl.BlockSpec((2, 3, 1, 4, 2, n, 128), lambda i: (0, 0, i, 0, 0, 0, 0)),
        ],
        out_specs=(smem, by_quarters, by_quarters, by_rows, by_rows),
    )(loss, fine_grad, coarse_grad, heads)


def solution(mesh):
    placed = (P(("grp", "mem"), None), P(("grp", "mem"), None), P(), P(), P(), P())
    return jax.shard_map(
        shards,
        mesh=mesh,
        in_specs=placed,
        out_specs=(P(), P(("grp", "mem"), None), P(("grp", "mem"), None), P(), P()),
        check_vma=False,
    )
```

time: 131 us -> 116 us (0.89)
  local copies, waits for them, and re-layouts: 7.76 us -> 0 us
  Pallas kernels: 119 us -> 114 us
  between operations: 3.85 us -> 1.93 us
    unnamed x8 -> x0, local copies, waits for them, and re-layouts: 7.76 us -> none
    pallas_call x1 -> x2, Pallas kernels: 119 us -> 114 us  [the longest x1 109 us: shards(): pl.pallas_call(kernel, out_shape=(jax.ShapeDtypeStruct((8, 128), F32), gr...]
where the time goes in v2:
time: 116 us
  Pallas kernels  114 us (98%)
  between operations  1.93 us (2%)
    pallas_call x1, Pallas kernels, shards(): pl.pallas_call(kernel, out_shape=(jax.ShapeDtypeStruct((8, 128), F32), gr...  109 us
    pallas_call x1, Pallas kernels, shards(): pl.pallas_call(place, grid=(4,), out_shape=(jax.ShapeDtypeStruct((1,), F3...  4.95 us

profile of v2, /device:TPU:1, one launch (start us, length us, event | category | flops | bytes accessed | tf_op | source)
XLA Modules:
  0.0 115.8 jit_solution(4409476972582642308)
XLA Ops:
  1.9 108.9 %shard_map.101 = (f32[8,128]{1,0:T(8,128)}, f32[192,768]{1,0:T(8,128)}, f32[192,768]{1,0:T(8,128)}, bf16[2,3,4,4,2,48,128]{6,5,4,3,2,1,0:T(8,128)(2,1)}) custom-call(bf16[192,768]{1,0:T(8,128)(2,1)} %fine_rows.1, bf16[192,768]{1,0:T(8,128)(2,1)} %coarse_rows.1, bf16[768,768]{1,0:T(8,128)(2,1)} %fine_head.1, bf16[768,768]{1,0:T(8,128)(2,1)} %coarse_head.1, ...), custom_call_target="tpu_custom_call" | custom-call | flops 21743271936 | bytes 18874368 | tf_op jit(solution)/shard_map/pallas_call | solution.py:527
  110.8 5.0 %shard_map.102 = (f32[1]{0:T(128)}, f32[192,768]{1,0:T(8,128)}, f32[192,768]{1,0:T(8,128)}, f32[768,768]{1,0:T(8,128)}, f32[768,768]{1,0:T(8,128)}) custom-call(f32[8,128]{1,0:T(8,128)} %get-tuple-element.9.refs_0_, f32[192,768]{1,0:T(8,128)} %get-tuple-element.10.refs_1_, f32[192,768]{1,0:T(8,128)} %get-tuple-element.11.refs_2_, ...), custom_call_target="tpu_custom_call" | custom-call | tf_op jit(solution)/shard_map/pallas_call | solution.py:547

commit v3 on v2

--- a/solution.py
+++ b/solution.py
@@ -51,7 +51,7 @@
 class Copies:
     def __init__(self, send_sem, recv_sem):
         self.send_sem, self.recv_sem = send_sem, recv_sem
-        self.made = {}
+        self.made, self.sent = {}, set()
 
     def start(self, name, src, dst, device):
         index = len(self.made)
@@ -74,12 +74,16 @@
         for name in names:
             self.made[name]().wait_recv()
 
+    def leave(self, *names):
+        for name in names:
+            self.sent.add(name)
+            self.made[name]().wait_send()
+
     def finish(self):
-        for make in self.made.values():
-            make().wait_send()
-
-
-N_COPIES = 128
+        self.leave(*[name for name in self.made if name not in self.sent])
+
+
+N_COPIES = 144
 ORDERS = (("x", "y", "z"), ("y", "z", "x"), ("z", "x", "y"))
 
 
@@ -113,7 +117,8 @@
     hop_in,
     own_sum,
     dp_keep,
-    grad_keep,
+    share_out,
+    share_in,
     part_out,
     part_in,
     quarter_out,
@@ -149,25 +154,29 @@
     h, shift = consts[0, 0:1, :], consts[1, 0:1, :]
     inputs = (fine_rows, coarse_rows)
 
-    def embed(which, far, part, head_ref):
-        at = pl.ds(part * half, half)
-        proj = dot(rows_keep[which, pl.ds(far * rows + part * half, half)], head_ref[...], NN)
+    far_rows = 4 * rows
+
+    def embed(which, start, keep_unit=False):
+        at = pl.ds(start, rows)
+        proj = dot(rows_keep[which, at], (fine_head, coarse_head)[which][...], NN)
         inv = lax.rsqrt(jnp.sum(proj * proj, axis=-1, keepdims=True) + EPS)
         unit = proj * inv
-        unit_keep[which, far, at] = unit
-        inv_keep[which, far, at] = inv
+        if keep_unit:
+            unit_keep[which] = unit
+        inv_keep[which, at] = inv
         return unit.astype(BF16)
 
-    for which in (0, 1):
-        rows_keep[which, pl.ds(0, rows)] = inputs[which][...]
+    rows_keep[0, slot(0)] = fine_rows[...]
+    rows_keep[1, pl.ds(far_rows, rows)] = coarse_rows[...]
     pl.semaphore_wait(barrier, len(partners))
     far_device = (here.other_hi, here.other_lo)
-    for part in (0, 1):
-        for which in (0, 1):
+
+    def to_far(which, start, end):
+        for p in (0, 1):
             copies.start(
-                f"z{which}{part}",
-                (rows_keep, which, pl.ds(part * half, half)),
-                (rows_keep, which, pl.ds(rows + part * half, half)),
+                f"z{which}{p}",
+                (rows_keep, which, pl.ds(start + p * half, half)),
+                (rows_keep, which, pl.ds(end + p * half, half)),
                 far_device[which],
             )
 
@@ -195,15 +204,16 @@
         copies.wait(tag + "++", tag + "--")
         copies.start(tag + "2s", (fine_all, at, slot(2)), (fine_all, at + 1, slot(2)), here.sibling)
 
-    for p in (0, 1):
-        fine_all[0, slot_half(0, p)] = embed(0, 0, p, fine_head)
-    send_both("fx", "x", fine_all, 0, (0, 1), (1, 0))
+    to_far(0, 0, far_rows)
+    send_both("fx", "x", rows_keep, 0, (0, 1), (1, 0))
+    to_far(1, far_rows, 0)
+    coarse_all[0, slot(0)] = embed(1, far_rows, True)
+    send_both("cy", "y", coarse_all, 0, (0, 1), (1, 0))
+    fine_all[0, slot(0)] = embed(0, 0, True)
     copies.start("fs", (fine_all, 0, slot(0)), (fine_all, 1, slot(0)), here.sibling)
-    for p in (0, 1):
-        coarse_all[0, slot_half(0, p)] = embed(1, 0, p, coarse_head)
-    send_both("cy", "y", coarse_all, 0, (0, 1), (1, 0))
 
     coarse_acc[...] = jnp.zeros_like(coarse_acc)
+    fine_acc[...] = jnp.zeros_like(fine_acc)
     loss_acc[...] = jnp.zeros_like(loss_acc)
 
     fine_emb = fine_all[0, slot(0)].astype(F32)
@@ -215,26 +225,29 @@
     own_sum[1] = delta * fine_emb
     diagonal = jnp.sum(2.0 * arg, axis=0, keepdims=True)
 
-    pass_plus("fx", "x", fine_all, 0)
+    pass_plus("fx", "x", rows_keep, 0)
+    pass_minus("fx", "x", rows_keep, 0)
     pass_plus("cy", "y", coarse_all, 0)
-    pass_minus("fx", "x", fine_all, 0)
     pass_minus("cy", "y", coarse_all, 0)
-    for p in (0, 1):
-        copies.wait(f"z0{p}")
-        fine_all[2, slot_half(0, p)] = embed(0, 1, p, fine_head)
-        for sign, step in (("+", 1), ("-", 3)):
-            copies.start(f"gx{sign}{p}", (fine_all, 2, slot_half(0, p)), (fine_all, 2, slot_half(-step, p)), here.along("x", step))
-        copies.wait(f"z1{p}")
-        coarse_all[1, slot_half(0, p)] = embed(1, 1, p, coarse_head)
-        for sign, step in (("+", 1), ("-", 3)):
-            copies.start(f"dy{sign}{p}", (coarse_all, 1, slot_half(0, p)), (coarse_all, 1, slot_half(-step, p)), here.along("y", step))
-    sib_near("fx", 0)
+
+    def near_fine(step, name):
+        fine_all[0, slot(step)] = embed(0, (step % 4) * rows)
+        copies.start(name, (fine_all, 0, slot(step)), (fine_all, 1, slot(step)), here.sibling)
+
+    copies.wait("fx+1")
+    near_fine(-1, "fx+s")
+    copies.wait("fx-0")
+    near_fine(1, "fx-s")
+    copies.wait("z00", "z01")
+    fine_all[2, slot(0)] = embed(0, far_rows)
+    send_both("gx", "x", fine_all, 2, (0, 1), (1, 0))
     copies.start("gs", (fine_all, 2, slot(0)), (fine_all, 3, slot(0)), here.sibling)
-    for which in (0, 1):
-        copies.start(f"rows{which}", (rows_keep, which, pl.ds(0, 2 * rows)), (rows_keep, which, pl.ds(2 * rows, 2 * rows)), here.sibling)
-    fine_acc[...] = jnp.zeros_like(fine_acc)
+    copies.wait("fx++", "fx--")
+    near_fine(2, "fx2s")
     copies.wait("cy+1", "cy-0", "cy++", "cy--")
-    sib_far("fx", 0)
+
+    def far_coarse(step):
+        coarse_all[1, slot(step)] = embed(1, (step % 4) * rows)
 
     def tile(fg, cg):
         cols = coarse_all[cg]
@@ -255,34 +268,41 @@
         coarse_acc[cg] += dot(jnp.concatenate(coefs, 0), fine_all[fg], TN)
 
     def to_sibling(k):
-        sib_out[k] = fine_acc[2 * k + 1].astype(BF16)
-        copies.start(f"sum_s{k}", (sib_out, k), (sib_in, k), here.sibling)
+        if k == 0:
+            copies.leave("sum_s1")
+        sib_out[...] = fine_acc[2 * k + 1].astype(BF16)
+        copies.start(f"sum_s{k}", (sib_out,), (sib_in, k), here.sibling)
 
     def ring_start(tag, axis, r, acc, a, other):
         def total(step, p):
             value = acc[a, slot_half(step, p)]
             return value if other is None else value + sib_in[other, slot_half(step, p)].astype(F32)
 
+        if r % 2 == 0:
+            earlier = {0: "f1", 2: "c0"}[r]
+            copies.leave(*[earlier + name for name in ("h+", "h-", "f+0", "f+1", "f-0", "f-1")])
         plus, minus = here.along(axis, 1), here.along(axis, 3)
-        half_out[r, upper] = total(2, 0).astype(BF16)
-        copies.start(tag + "h+", (half_out, r, upper), (half_in, r, upper), plus)
-        half_out[r, lower] = total(2, 1).astype(BF16)
-        copies.start(tag + "h-", (half_out, r, lower), (half_in, r, lower), minus)
-        full_out[r, 0, lower] = total(1, 1).astype(BF16)
-        copies.start(tag + "f+1", (full_out, r, 0, lower), (full_in, r, 0, lower), plus)
-        full_out[r, 1, upper] = total(3, 0).astype(BF16)
-        copies.start(tag + "f-0", (full_out, r, 1, upper), (full_in, r, 1, upper), minus)
-        if other is not None:
-            for step, p in ((1, 0), (3, 1), (0, 0), (0, 1)):
-                acc[a, slot_half(step, p)] = total(step, p)
+        half_out[r // 2, upper] = total(2, 0).astype(BF16)
+        copies.start(tag + "h+", (half_out, r // 2, upper), (half_in, r, upper), plus)
+        half_out[r // 2, lower] = total(2, 1).astype(BF16)
+        copies.start(tag + "h-", (half_out, r // 2, lower), (half_in, r, lower), minus)
+        full_out[r // 2, 0, lower] = total(1, 1).astype(BF16)
+        copies.start(tag + "f+1", (full_out, r // 2, 0, lower), (full_in, r, 0, lower), plus)
+        full_out[r // 2, 1, upper] = total(3, 0).astype(BF16)
+        copies.start(tag + "f-0", (full_out, r // 2, 1, upper), (full_in, r, 1, upper), minus)
+
+    def ring_own(acc, a, other):
+        for step, p in ((1, 0), (3, 1), (0, 0), (0, 1)):
+            at = slot_half(step, p)
+            acc[a, at] += sib_in[other, at].astype(F32)
 
     def ring_middle(tag, axis, r, acc, a):
         copies.wait(tag + "h+")
-        full_out[r, 0, upper] = (acc[a, slot_half(1, 0)] + half_in[r, upper].astype(F32)).astype(BF16)
-        copies.start(tag + "f+0", (full_out, r, 0, upper), (full_in, r, 0, upper), here.along(axis, 1))
+        full_out[r // 2, 0, upper] = (acc[a, slot_half(1, 0)] + half_in[r, upper].astype(F32)).astype(BF16)
+        copies.start(tag + "f+0", (full_out, r // 2, 0, upper), (full_in, r, 0, upper), here.along(axis, 1))
         copies.wait(tag + "h-")
-        full_out[r, 1, lower] = (acc[a, slot_half(3, 1)] + half_in[r, lower].astype(F32)).astype(BF16)
-        copies.start(tag + "f-1", (full_out, r, 1, lower), (full_in, r, 1, lower), here.along(axis, 3))
+        full_out[r // 2, 1, lower] = (acc[a, slot_half(3, 1)] + half_in[r, lower].astype(F32)).astype(BF16)
+        copies.start(tag + "f-1", (full_out, r // 2, 1, lower), (full_in, r, 1, lower), here.along(axis, 3))
 
     def ring_end(tag, r, acc, a):
         copies.wait(tag + "f+0", tag + "f+1", tag + "f-0", tag + "f-1")
@@ -295,36 +315,43 @@
     def step(t, carry):
         @pl.when(t == 1)
         def _():
+            copies.wait("z10", "z11")
+            send_both("dy", "y", rows_keep, 1, (0, 1), (1, 0))
             pass_plus("gx", "x", fine_all, 2)
-            pass_plus("dy", "y", coarse_all, 1)
+            pass_minus("gx", "x", fine_all, 2)
             copies.wait("fs", "fx+s", "fx-s", "fx2s")
 
         @pl.when(t == 2)
         def _():
-            pass_minus("gx", "x", fine_all, 2)
-            pass_minus("dy", "y", coarse_all, 1)
             sib_near("gx", 2)
+            pass_plus("dy", "y", rows_keep, 1)
+            pass_minus("dy", "y", rows_keep, 1)
+            far_coarse(0)
             sib_far("gx", 2)
 
         @pl.when(t == 3)
         def _():
-            copies.wait("gs", "gx+s", "gx-s", "gx2s")
+            copies.wait("gs", "gx+s", "gx-s", "gx2s", "dy+1", "dy-0")
+            far_coarse(-1)
+            far_coarse(1)
 
         @pl.when(t == 4)
         def _():
-            ring_start("c0", "y", 2, coarse_acc, 0, None)
-            copies.wait("dy+1", "dy-0", "dy++", "dy--")
+            ring_start("c0", "y", 3, coarse_acc, 0, None)
+            copies.wait("dy++", "dy--")
+            far_coarse(2)
 
         @pl.when(t == 5)
         def _():
             to_sibling(1)
-            ring_middle("c0", "y", 2, coarse_acc, 0)
+            ring_middle("c0", "y", 3, coarse_acc, 0)
 
         @pl.when(t == 6)
         def _():
             copies.wait("sum_s1")
             ring_start("f1", "x", 1, fine_acc, 2, 1)
-            own_sum[1] += ring_end("c0", 2, coarse_acc, 0)
+            ring_own(fine_acc, 2, 1)
+            own_sum[1] += ring_end("c0", 3, coarse_acc, 0)
 
         @pl.when(t == 7)
         def _():
@@ -337,31 +364,44 @@
 
     lax.fori_loop(0, 8, step, 0)
 
-    def back(which, far, value):
-        unit, inv = unit_keep[which, far], inv_keep[which, far]
+    def back(which, value, unit, inv):
         grad = value * h
         inner = jnp.sum(unit * grad, axis=-1, keepdims=True)
         return (inv * (grad - unit * inner)).astype(BF16)
 
-    def keep(which, far, value):
-        dp = back(which, far, value)
+    def keep(which, start, value, emb):
+        at = pl.ds(start, rows)
+        dp = back(which, value, emb.astype(F32), inv_keep[which, at])
         for i in (0, 1):
-            dp_keep[which, i, pl.ds(far * rows, rows)] = dp[:, i * wide : (i + 1) * wide]
-
-    def dp_to_sibling(which):
-        other = 1 - here.core
-        copies.start(f"dp{which}", (dp_keep, which, other, pl.ds(0, 2 * rows)), (dp_keep, which, other, pl.ds(2 * rows, 2 * rows)), here.sibling)
-
-    def grad_to_out(which, value, head_ref, out):
-        grad_keep[which] = dot(back(which, 0, value), head_ref[...], NT)
-        return pltpu.make_async_copy(grad_keep.at[which], out, local_sem.at[which])
-
+            dp_keep[which, i, at] = dp[:, i * wide : (i + 1) * wide]
+
+    def grad_to_out(which, start, value, head_ref, out):
+        dp = back(which, value, unit_keep[which], inv_keep[which, pl.ds(start, rows)])
+        fine_acc[2 * which + 1, slot(0)] = dot(dp, head_ref[...], NT)
+        return pltpu.make_async_copy(fine_acc.at[2 * which + 1, slot(0)], out, local_sem.at[which])
+
+    core = here.core
+    other = 1 - core
+
+    ring_start("c1", "y", 2, coarse_acc, 1, None)
     copies.wait("sum_s0")
-    ring_start("f0", "x", 0, fine_acc, 0, 0)
-    ring_start("c1", "y", 3, coarse_acc, 1, None)
+    fine_acc[0] += sib_in[0].astype(F32)
+    ring_start("f0", "x", 0, fine_acc, 0, None)
     value = ring_end("f1", 1, fine_acc, 2)
     hop(0, value)
-    keep(0, 1, value)
+    keep(0, far_rows, value, fine_all[2, slot(0)])
+    keep(1, far_rows, own_sum[1], coarse_all[0, slot(0)])
+    for i in range(4):
+        value = fine_acc[0, slot(i)]
+        keep(0, i * rows, value + own_sum[0] if i == 0 else value, fine_all[0, slot(i)])
+    share_out[0] = dot(rows_keep[0], dp_keep[0, other], TN).astype(BF16)
+    for i in range(4):
+        keep(1, i * rows, coarse_acc[1, slot(i)], coarse_all[1, slot(i)])
+    copies.start("part_s0", (share_out, 0), (share_in, 0), here.sibling)
+    share_out[1] = dot(rows_keep[1], dp_keep[1, other], TN).astype(BF16)
+    copies.start("part_s1", (share_out, 1), (share_in, 1), here.sibling)
+    ring_middle("c1", "y", 2, coarse_acc, 1)
+    ring_middle("f0", "x", 0, fine_acc, 0)
 
     loss = loss_acc[:, 0:128]
     for i in range(1, width // 128):
@@ -385,26 +425,12 @@
         for d in (1, 2, 3):
             copies.start(f"loss{r}{d}", (loss_parts, r, place), (loss_parts, r, place), here.along(axis, d))
 
-    ring_middle("f0", "x", 0, fine_acc, 0)
-    ring_middle("c1", "y", 3, coarse_acc, 1)
-    loss_round(1, "x", here.x)
-    keep(1, 0, own_sum[1])
-    value = ring_end("f0", 0, fine_acc, 0) + own_sum[0]
-    own_sum[0] = value
-    keep(0, 0, value)
-    dp_to_sibling(0)
-    value = ring_end("c1", 3, coarse_acc, 1)
-    keep(1, 1, value)
-    dp_to_sibling(1)
-    hop(1, value)
-    loss_round(2, "y", here.y)
-
     place = {"x": here.x, "y": here.y, "z": here.z}
-    core = here.core
     n = rows // 4
     for which in (0, 1):
-        copies.wait(f"rows{which}", f"dp{which}")
         value = dot(rows_keep[which], dp_keep[which, core], TN)
+        copies.wait(f"part_s{which}")
+        value = value + share_in[which].astype(F32)
         for q in range(3):
             for j in range(4):
                 part_out[q, j, which] = value[j * rows : (j + 1) * rows, q * 128 : (q + 1) * 128].astype(BF16)
@@ -412,12 +438,8 @@
         for q, (first, _, _) in enumerate(ORDERS):
             copies.start(f"part{q}{d}", (part_out, q, (place[first] + d) % 4), (part_in, q, d - 1), here.along(first, d))
 
-    copies.wait("hop0")
-    fine_copy = grad_to_out(0, own_sum[0] + hop_in[0].astype(F32), fine_head, fine_grad_out)
-    fine_copy.start()
-    copies.wait("hop1")
-    coarse_copy = grad_to_out(1, own_sum[1] + hop_in[1].astype(F32), coarse_head, coarse_grad_out)
-    coarse_copy.start()
+    loss_round(1, "x", here.x)
+    hop(1, ring_end("c1", 2, coarse_acc, 1))
 
     for q, (first, second, _) in enumerate(ORDERS):
         copies.wait(*[f"part{q}{d}" for d in (1, 2, 3)])
@@ -428,7 +450,8 @@
             quarter_out[q, j] = value[:, j * n : (j + 1) * n].astype(BF16)
         for d in (1, 3, 2):
             copies.start(f"quarter{q}{d}", (quarter_out, q, (place[second] + d) % 4), (quarter_in, q, d - 1), here.along(second, d))
-    loss_round(3, "z", here.z)
+    loss_round(2, "y", here.y)
+    own_sum[0] += ring_end("f0", 0, fine_acc, 0)
     for q, (_, second, third) in enumerate(ORDERS):
         copies.wait(*[f"quarter{q}{d}" for d in (1, 2, 3)])
         value = quarter_out[q, place[second]].astype(F32)
@@ -438,6 +461,7 @@
         mine = (column, q, place[third])
         for d in (1, 3, 2):
             copies.start(f"column{q}{d}", mine, mine, here.along(third, d))
+    loss_round(3, "z", here.z)
     for q, (first, second, third) in enumerate(ORDERS):
         copies.wait(*[f"column{q}{d}" for d in (1, 2, 3)])
         value = column[q, 0].astype(F32)
@@ -447,18 +471,29 @@
         mine = (heads, core, q, place[first], place[second])
         for d in (1, 3, 2):
             copies.start(f"back{q}{d}", mine, mine, here.along(second, d))
-    loss_out[...] = loss_round(4, None, None)
+    copies.wait("hop0")
+    fine_copy = grad_to_out(0, 0, own_sum[0] + hop_in[0].astype(F32), fine_head, fine_grad_out)
+    fine_copy.start()
     for q, (first, second, _) in enumerate(ORDERS):
         copies.wait(*[f"back{q}{d}" for d in (1, 2, 3)])
         mine = (heads, core, q, place[first])
         for d in (1, 3, 2):
             copies.start(f"spread{q}{d}", mine, mine, here.along(first, d))
-    for q in range(3):
-        copies.wait(*[f"spread{q}{d}" for d in (1, 2, 3)])
-        copies.start(f"share{q}", (heads, core, q), (heads, core, q), here.sibling)
+    for q, (first, _, _) in enumerate(ORDERS):
+        mine = (heads, core, q, place[first])
+        copies.start(f"share{q}0", mine, mine, here.sibling)
+    copies.wait("hop1")
+    coarse_copy = grad_to_out(1, far_rows, own_sum[1] + hop_in[1].astype(F32), coarse_head, coarse_grad_out)
+    coarse_copy.start()
+    loss_out[...] = loss_round(4, None, None)
+    for d in (1, 3, 2):
+        for q, (first, _, _) in enumerate(ORDERS):
+            copies.wait(f"spread{q}{d}")
+            got = (heads, core, q, (place[first] + 4 - d) % 4)
+            copies.start(f"share{q}{d}", got, got, here.sibling)
     mine_copy = pltpu.make_async_copy(heads.at[core], heads_out.at[core], local_sem.at[2])
     mine_copy.start()
-    copies.wait("share0", "share1", "share2")
+    copies.wait(*[f"share{q}{d}" for q in range(3) for d in range(4)])
     other_copy = pltpu.make_async_copy(heads.at[1 - core], heads_out.at[1 - core], local_sem.at[3])
     other_copy.start()
     copies.finish()
@@ -493,22 +528,23 @@
         VMEM((2, 4 * rows, width), BF16),
         VMEM((4, 4 * rows, width), F32),
         VMEM((2, 4 * rows, width), F32),
-        VMEM((2, 2, rows, width), F32),
-        VMEM((2, 2, rows, 1), F32),
-        VMEM((2, 4 * rows, width), BF16),
+        VMEM((2, rows, width), F32),
+        VMEM((2, 5 * rows, 1), F32),
+        VMEM((2, 5 * rows, width), BF16),
         VMEM((2, 8, width), F32),
         VMEM((8, width), F32),
+        VMEM((4 * rows, width), BF16),
         VMEM((2, 4 * rows, width), BF16),
-        VMEM((2, 4 * rows, width), BF16),
+        VMEM((2, rows, width), BF16),
         VMEM((4, rows, width), BF16),
-        VMEM((4, rows, width), BF16),
-        VMEM((4, 2, rows, width), BF16),
+        VMEM((2, 2, rows, width), BF16),
         VMEM((4, 2, rows, width), BF16),
         VMEM((2, rows, width), BF16),
         VMEM((2, rows, width), BF16),
         VMEM((2, rows, width), F32),
-        VMEM((2, 2, 4 * rows, wide), BF16),
-        VMEM((2, rows, width), F32),
+        VMEM((2, 2, 5 * rows, wide), BF16),
+        VMEM((2, width, wide), BF16),
+        VMEM((2, width, wide), BF16),
         VMEM((3, 4, 2, rows, 128), BF16),
         VMEM((3, 3, 2, rows, 128), BF16),
         VMEM((3, 4, 2, n, 128), BF16),

time: 116 us -> 109 us (0.940)
  Pallas kernels: 114 us -> 106 us
    pallas_call x1, Pallas kernels: 109 us -> 101 us  [shards(): pl.pallas_call(kernel, out_shape=(jax.ShapeDtypeStruct((8, 128), F32), gr...]
where the time goes in v3:
time: 109 us; the launch traced here: 108 us
  Pallas kernels  106 us (97%)
  between operations  1.93 us (2%)
    pallas_call x1, Pallas kernels, shards(): pl.pallas_call(kernel, out_shape=(jax.ShapeDtypeStruct((8, 128), F32), gr...  101 us
    pallas_call x1, Pallas kernels, shards(): pl.pallas_call(place, grid=(4,), out_shape=(jax.ShapeDtypeStruct((1,), F3...  4.95 us

profile of v3, /device:TPU:1, one launch (start us, length us, event | category | flops | bytes accessed | tf_op | source)
XLA Modules:
  0.0 108.3 jit_solution(7133349067311026089)
XLA Ops:
  1.9 101.4 %shard_map.101 = (f32[8,128]{1,0:T(8,128)}, f32[192,768]{1,0:T(8,128)}, f32[192,768]{1,0:T(8,128)}, bf16[2,3,4,4,2,48,128]{6,5,4,3,2,1,0:T(8,128)(2,1)}) custom-call(bf16[192,768]{1,0:T(8,128)(2,1)} %fine_rows.1, bf16[192,768]{1,0:T(8,128)(2,1)} %coarse_rows.1, bf16[768,768]{1,0:T(8,128)(2,1)} %fine_head.1, bf16[768,768]{1,0:T(8,128)(2,1)} %coarse_head.1, ...), custom_call_target="tpu_custom_call" | custom-call | flops 21743271936 | bytes 18874368 | tf_op jit(solution)/shard_map/pallas_call | solution.py:563
  103.3 5.0 %shard_map.102 = (f32[1]{0:T(128)}, f32[192,768]{1,0:T(8,128)}, f32[192,768]{1,0:T(8,128)}, f32[768,768]{1,0:T(8,128)}, f32[768,768]{1,0:T(8,128)}) custom-call(f32[8,128]{1,0:T(8,128)} %get-tuple-element.9.refs_0_, f32[192,768]{1,0:T(8,128)} %get-tuple-element.10.refs_1_, f32[192,768]{1,0:T(8,128)} %get-tuple-element.11.refs_2_, ...), custom_call_target="tpu_custom_call" | custom-call | tf_op jit(solution)/shard_map/pallas_call | solution.py:583

commit v4 on v3

--- a/solution.py
+++ b/solution.py
@@ -234,13 +234,13 @@
         fine_all[0, slot(step)] = embed(0, (step % 4) * rows)
         copies.start(name, (fine_all, 0, slot(step)), (fine_all, 1, slot(step)), here.sibling)
 
+    copies.wait("z00", "z01")
+    fine_all[2, slot(0)] = embed(0, far_rows)
+    send_both("gx", "x", fine_all, 2, (0, 1), (1, 0))
     copies.wait("fx+1")
     near_fine(-1, "fx+s")
     copies.wait("fx-0")
     near_fine(1, "fx-s")
-    copies.wait("z00", "z01")
-    fine_all[2, slot(0)] = embed(0, far_rows)
-    send_both("gx", "x", fine_all, 2, (0, 1), (1, 0))
     copies.start("gs", (fine_all, 2, slot(0)), (fine_all, 3, slot(0)), here.sibling)
     copies.wait("fx++", "fx--")
     near_fine(2, "fx2s")
@@ -251,7 +251,7 @@
 
     def tile(fg, cg):
         cols = coarse_all[cg]
-        n = 256
+        n = 2 * rows
         coefs = []
         for j in range(4 * rows // n):
             at = pl.ds(j * n, n)
@@ -262,7 +262,8 @@
             p = [rest[i * eighth : (i + 1) * eighth] for i in range(8)]
             p = ((p[0] * p[1]) * (p[2] * p[3])) * ((p[4] * p[5]) * (p[6] * p[7]))
             p = jnp.log(p * (1.0 / 256.0))
-            loss_acc[...] -= (p[0:8] + p[8:16]) + (p[16:24] + p[24:32])
+            for i in range(0, eighth, 8):
+                loss_acc[...] -= p[i : i + 8]
             fine_acc[fg, at] += dot(coef, cols, NN)
             coefs.append(coef)
         coarse_acc[cg] += dot(jnp.concatenate(coefs, 0), fine_all[fg], TN)
@@ -315,19 +316,19 @@
     def step(t, carry):
         @pl.when(t == 1)
         def _():
+            pass_plus("gx", "x", fine_all, 2)
+            pass_minus("gx", "x", fine_all, 2)
             copies.wait("z10", "z11")
             send_both("dy", "y", rows_keep, 1, (0, 1), (1, 0))
-            pass_plus("gx", "x", fine_all, 2)
-            pass_minus("gx", "x", fine_all, 2)
             copies.wait("fs", "fx+s", "fx-s", "fx2s")
 
         @pl.when(t == 2)
         def _():
             sib_near("gx", 2)
+            far_coarse(0)
+            sib_far("gx", 2)
             pass_plus("dy", "y", rows_keep, 1)
             pass_minus("dy", "y", rows_keep, 1)
-            far_coarse(0)
-            sib_far("gx", 2)
 
         @pl.when(t == 3)
         def _():
@@ -344,14 +345,13 @@
         @pl.when(t == 5)
         def _():
             to_sibling(1)
-            ring_middle("c0", "y", 3, coarse_acc, 0)
 
         @pl.when(t == 6)
         def _():
             copies.wait("sum_s1")
             ring_start("f1", "x", 1, fine_acc, 2, 1)
             ring_own(fine_acc, 2, 1)
-            own_sum[1] += ring_end("c0", 3, coarse_acc, 0)
+            ring_middle("c0", "y", 3, coarse_acc, 0)
 
         @pl.when(t == 7)
         def _():
@@ -364,19 +364,20 @@
 
     lax.fori_loop(0, 8, step, 0)
 
-    def back(which, value, unit, inv):
-        grad = value * h
-        inner = jnp.sum(unit * grad, axis=-1, keepdims=True)
-        return (inv * (grad - unit * inner)).astype(BF16)
-
-    def keep(which, start, value, emb):
-        at = pl.ds(start, rows)
-        dp = back(which, value, emb.astype(F32), inv_keep[which, at])
-        for i in (0, 1):
-            dp_keep[which, i, at] = dp[:, i * wide : (i + 1) * wide]
+    def back(value, unit, inv):
+        inner = jnp.sum(unit * value, axis=-1, keepdims=True)
+        return ((inv * h) * (value - unit * inner)).astype(BF16)
+
+    def keep(which, start, value_at, buf, a, first):
+        n = 32
+        for i in range(0, rows, n):
+            at = pl.ds(start + i, n)
+            dp = back(value_at(i, n), buf[a, pl.ds(first + i, n)].astype(F32), inv_keep[which, at])
+            for side in (0, 1):
+                dp_keep[which, side, at] = dp[:, side * wide : (side + 1) * wide]
 
     def grad_to_out(which, start, value, head_ref, out):
-        dp = back(which, value, unit_keep[which], inv_keep[which, pl.ds(start, rows)])
+        dp = back(value, unit_keep[which], inv_keep[which, pl.ds(start, rows)])
         fine_acc[2 * which + 1, slot(0)] = dot(dp, head_ref[...], NT)
         return pltpu.make_async_copy(fine_acc.at[2 * which + 1, slot(0)], out, local_sem.at[which])
 
@@ -385,22 +386,28 @@
 
     ring_start("c1", "y", 2, coarse_acc, 1, None)
     copies.wait("sum_s0")
-    fine_acc[0] += sib_in[0].astype(F32)
+    for i in range(4):
+        fine_acc[0, slot(i)] += sib_in[0, slot(i)].astype(F32)
     ring_start("f0", "x", 0, fine_acc, 0, None)
+    own_sum[1] += ring_end("c0", 3, coarse_acc, 0)
+    keep(1, far_rows, lambda i, n: own_sum[1, pl.ds(i, n)], coarse_all, 0, 0)
+    keep(1, 0, lambda i, n: coarse_acc[1, pl.ds(i, n)], coarse_all, 1, 0)
+    keep(1, rows, lambda i, n: coarse_acc[1, pl.ds(rows + i, n)], coarse_all, 1, rows)
+    keep(1, 2 * rows, lambda i, n: coarse_acc[1, pl.ds(2 * rows + i, n)], coarse_all, 1, 2 * rows)
+    keep(1, 3 * rows, lambda i, n: coarse_acc[1, pl.ds(3 * rows + i, n)], coarse_all, 1, 3 * rows)
+    share_out[1] = dot(rows_keep[1], dp_keep[1, other], TN).astype(BF16)
+    keep(0, 0, lambda i, n: fine_acc[0, pl.ds(i, n)] + own_sum[0, pl.ds(i, n)], fine_all, 0, 0)
+    keep(0, rows, lambda i, n: fine_acc[0, pl.ds(rows + i, n)], fine_all, 0, rows)
+    keep(0, 2 * rows, lambda i, n: fine_acc[0, pl.ds(2 * rows + i, n)], fine_all, 0, 2 * rows)
+    keep(0, 3 * rows, lambda i, n: fine_acc[0, pl.ds(3 * rows + i, n)], fine_all, 0, 3 * rows)
+    copies.start("part_s1", (share_out, 1), (share_in, 1), here.sibling)
+    ring_middle("c1", "y", 2, coarse_acc, 1)
     value = ring_end("f1", 1, fine_acc, 2)
     hop(0, value)
-    keep(0, far_rows, value, fine_all[2, slot(0)])
-    keep(1, far_rows, own_sum[1], coarse_all[0, slot(0)])
-    for i in range(4):
-        value = fine_acc[0, slot(i)]
-        keep(0, i * rows, value + own_sum[0] if i == 0 else value, fine_all[0, slot(i)])
+    fine_acc[2, slot(0)] = value
+    keep(0, far_rows, lambda i, n: fine_acc[2, pl.ds(i, n)], fine_all, 2, 0)
     share_out[0] = dot(rows_keep[0], dp_keep[0, other], TN).astype(BF16)
-    for i in range(4):
-        keep(1, i * rows, coarse_acc[1, slot(i)], coarse_all[1, slot(i)])
     copies.start("part_s0", (share_out, 0), (share_in, 0), here.sibling)
-    share_out[1] = dot(rows_keep[1], dp_keep[1, other], TN).astype(BF16)
-    copies.start("part_s1", (share_out, 1), (share_in, 1), here.sibling)
-    ring_middle("c1", "y", 2, coarse_acc, 1)
     ring_middle("f0", "x", 0, fine_acc, 0)
 
     loss = loss_acc[:, 0:128]
@@ -427,7 +434,7 @@
 
     place = {"x": here.x, "y": here.y, "z": here.z}
     n = rows // 4
-    for which in (0, 1):
+    for which in (1, 0):
         value = dot(rows_keep[which], dp_keep[which, core], TN)
         copies.wait(f"part_s{which}")
         value = value + share_in[which].astype(F32)
@@ -486,15 +493,15 @@
     coarse_copy = grad_to_out(1, far_rows, own_sum[1] + hop_in[1].astype(F32), coarse_head, coarse_grad_out)
     coarse_copy.start()
     loss_out[...] = loss_round(4, None, None)
+    mine_copy = pltpu.make_async_copy(heads.at[core], heads_out.at[core], local_sem.at[2])
     for d in (1, 3, 2):
         for q, (first, _, _) in enumerate(ORDERS):
             copies.wait(f"spread{q}{d}")
             got = (heads, core, q, (place[first] + 4 - d) % 4)
             copies.start(f"share{q}{d}", got, got, here.sibling)
-    mine_copy = pltpu.make_async_copy(heads.at[core], heads_out.at[core], local_sem.at[2])
     mine_copy.start()
     copies.wait(*[f"share{q}{d}" for q in range(3) for d in range(4)])
-    other_copy = pltpu.make_async_copy(heads.at[1 - core], heads_out.at[1 - core], local_sem.at[3])
+    other_copy = pltpu.make_async_copy(heads.at[other], heads_out.at[other], local_sem.at[3])
     other_copy.start()
     copies.finish()
     fine_copy.wait()
@@ -507,14 +514,15 @@
     loss[0] = jnp.sum(loss_in[...]) * (1.0 / pairs)
     fine_grad[...] = fine_in[...]
     coarse_grad[...] = coarse_in[...]
-    halves, parts, _, pieces, _, n, lanes = heads.shape
+    halves, parts, bands, pieces, _, n, lanes = heads.shape
     for side in range(halves):
         for q in range(parts):
             cols = pl.ds((side * parts + q) * lanes, lanes)
-            for j in range(pieces):
-                at = pl.ds(j * n, n)
-                fine_head_grad[at, cols] = heads[side, q, 0, j, 0].astype(F32)
-                coarse_head_grad[at, cols] = heads[side, q, 0, j, 1].astype(F32)
+            for k in range(bands):
+                for j in range(pieces):
+                    at = pl.ds((k * pieces + j) * n, n)
+                    fine_head_grad[at, cols] = heads[side, q, k, j, 0].astype(F32)
+                    coarse_head_grad[at, cols] = heads[side, q, k, j, 1].astype(F32)
 
 
 def shards(fine_rows, coarse_rows, fine_head, coarse_head, log_scale, bias):
@@ -578,19 +586,19 @@
     def place(*refs):
         place_results(float(tokens) ** 2, *refs)
 
-    by_rows = pl.BlockSpec((rows, width), lambda i: (i, 0))
-    by_quarters = pl.BlockSpec((n, width), lambda i: (i, 0))
+    by_rows = pl.BlockSpec((rows * 2, width), lambda i: (i, 0))
+    by_halves = pl.BlockSpec((rows // 2, width), lambda i: (i, 0))
     return pl.pallas_call(
         place,
-        grid=(4,),
+        grid=(2,),
         out_shape=(jax.ShapeDtypeStruct((1,), F32), grad, grad, head, head),
         in_specs=[
             pl.BlockSpec((8, 128), lambda i: (0, 0)),
-            by_quarters,
-            by_quarters,
-            pl.BlockSpec((2, 3, 1, 4, 2, n, 128), lambda i: (0, 0, i, 0, 0, 0, 0)),
+            by_halves,
+            by_halves,
+            pl.BlockSpec((2, 3, 2, 4, 2, n, 128), lambda i: (0, 0, i, 0, 0, 0, 0)),
         ],
-        out_specs=(smem, by_quarters, by_quarters, by_rows, by_rows),
+        out_specs=(smem, by_halves, by_halves, by_rows, by_rows),
     )(loss, fine_grad, coarse_grad, heads)
 
 

time: 109 us -> 104 us (0.954)
  Pallas kernels: 106 us -> 102 us
    pallas_call x1, Pallas kernels: 101 us -> 98.1 us  [shards(): pl.pallas_call(kernel, out_shape=(jax.ShapeDtypeStruct((8, 128), F32), gr...]
where the time goes in v4:
time: 104 us
  Pallas kernels  102 us (98%)
  between operations  1.93 us (2%)
    pallas_call x1, Pallas kernels, shards(): pl.pallas_call(kernel, out_shape=(jax.ShapeDtypeStruct((8, 128), F32), gr...  98.1 us
    pallas_call x1, Pallas kernels, shards(): pl.pallas_call(place, grid=(2,), out_shape=(jax.ShapeDtypeStruct((1,), F3...  4.1 us

profile of v4, /device:TPU:1, one launch (start us, length us, event | category | flops | bytes accessed | tf_op | source)
XLA Modules:
  0.0 104.1 jit_solution(576830119023454060)
XLA Ops:
  1.9 98.1 %shard_map.101 = (f32[8,128]{1,0:T(8,128)}, f32[192,768]{1,0:T(8,128)}, f32[192,768]{1,0:T(8,128)}, bf16[2,3,4,4,2,48,128]{6,5,4,3,2,1,0:T(8,128)(2,1)}) custom-call(bf16[192,768]{1,0:T(8,128)(2,1)} %fine_rows.1, bf16[192,768]{1,0:T(8,128)(2,1)} %coarse_rows.1, bf16[768,768]{1,0:T(8,128)(2,1)} %fine_head.1, bf16[768,768]{1,0:T(8,128)(2,1)} %coarse_head.1, ...), custom_call_target="tpu_custom_call" | custom-call | flops 21743271936 | bytes 18874368 | tf_op jit(solution)/shard_map/pallas_call | solution.py:571
  100.0 4.1 %shard_map.102 = (f32[1]{0:T(128)}, f32[192,768]{1,0:T(8,128)}, f32[192,768]{1,0:T(8,128)}, f32[768,768]{1,0:T(8,128)}, f32[768,768]{1,0:T(8,128)}) custom-call(f32[8,128]{1,0:T(8,128)} %get-tuple-element.9.refs_0_, f32[192,768]{1,0:T(8,128)} %get-tuple-element.10.refs_1_, f32[192,768]{1,0:T(8,128)} %get-tuple-element.11.refs_2_, ...), custom_call_target="tpu_custom_call" | custom-call | tf_op jit(solution)/shard_map/pallas_call | solution.py:591

commit v5 on v4

--- a/solution.py
+++ b/solution.py
@@ -309,9 +309,10 @@
         copies.wait(tag + "f+0", tag + "f+1", tag + "f-0", tag + "f-1")
         return acc[a, slot(0)] + full_in[r, 0].astype(F32) + full_in[r, 1].astype(F32)
 
-    def hop(which, value):
-        hop_out[which] = value.astype(BF16)
-        copies.start(f"hop{which}", (hop_out, which), (hop_in, which), far_device[which])
+    def hop(which, *parts):
+        for p in parts:
+            at = pl.ds(p * half, half)
+            copies.start(f"hop{which}{p}", (hop_out, which, at), (hop_in, which, at), far_device[which])
 
     def step(t, carry):
         @pl.when(t == 1)
@@ -395,6 +396,10 @@
     keep(1, rows, lambda i, n: coarse_acc[1, pl.ds(rows + i, n)], coarse_all, 1, rows)
     keep(1, 2 * rows, lambda i, n: coarse_acc[1, pl.ds(2 * rows + i, n)], coarse_all, 1, 2 * rows)
     keep(1, 3 * rows, lambda i, n: coarse_acc[1, pl.ds(3 * rows + i, n)], coarse_all, 1, 3 * rows)
+    value = ring_end("f1", 1, fine_acc, 2)
+    hop_out[0] = value.astype(BF16)
+    fine_acc[2, slot(0)] = value
+    hop(0, 0, 1)
     share_out[1] = dot(rows_keep[1], dp_keep[1, other], TN).astype(BF16)
     keep(0, 0, lambda i, n: fine_acc[0, pl.ds(i, n)] + own_sum[0, pl.ds(i, n)], fine_all, 0, 0)
     keep(0, rows, lambda i, n: fine_acc[0, pl.ds(rows + i, n)], fine_all, 0, rows)
@@ -402,13 +407,9 @@
     keep(0, 3 * rows, lambda i, n: fine_acc[0, pl.ds(3 * rows + i, n)], fine_all, 0, 3 * rows)
     copies.start("part_s1", (share_out, 1), (share_in, 1), here.sibling)
     ring_middle("c1", "y", 2, coarse_acc, 1)
-    value = ring_end("f1", 1, fine_acc, 2)
-    hop(0, value)
-    fine_acc[2, slot(0)] = value
     keep(0, far_rows, lambda i, n: fine_acc[2, pl.ds(i, n)], fine_all, 2, 0)
     share_out[0] = dot(rows_keep[0], dp_keep[0, other], TN).astype(BF16)
     copies.start("part_s0", (share_out, 0), (share_in, 0), here.sibling)
-    ring_middle("f0", "x", 0, fine_acc, 0)
 
     loss = loss_acc[:, 0:128]
     for i in range(1, width // 128):
@@ -446,7 +447,6 @@
             copies.start(f"part{q}{d}", (part_out, q, (place[first] + d) % 4), (part_in, q, d - 1), here.along(first, d))
 
     loss_round(1, "x", here.x)
-    hop(1, ring_end("c1", 2, coarse_acc, 1))
 
     for q, (first, second, _) in enumerate(ORDERS):
         copies.wait(*[f"part{q}{d}" for d in (1, 2, 3)])
@@ -458,7 +458,9 @@
         for d in (1, 3, 2):
             copies.start(f"quarter{q}{d}", (quarter_out, q, (place[second] + d) % 4), (quarter_in, q, d - 1), here.along(second, d))
     loss_round(2, "y", here.y)
-    own_sum[0] += ring_end("f0", 0, fine_acc, 0)
+    hop_out[1] = ring_end("c1", 2, coarse_acc, 1).astype(BF16)
+    hop(1, 0)
+    ring_middle("f0", "x", 0, fine_acc, 0)
     for q, (_, second, third) in enumerate(ORDERS):
         copies.wait(*[f"quarter{q}{d}" for d in (1, 2, 3)])
         value = quarter_out[q, place[second]].astype(F32)
@@ -468,6 +470,7 @@
         mine = (column, q, place[third])
         for d in (1, 3, 2):
             copies.start(f"column{q}{d}", mine, mine, here.along(third, d))
+    hop(1, 1)
     loss_round(3, "z", here.z)
     for q, (first, second, third) in enumerate(ORDERS):
         copies.wait(*[f"column{q}{d}" for d in (1, 2, 3)])
@@ -478,7 +481,8 @@
         mine = (heads, core, q, place[first], place[second])
         for d in (1, 3, 2):
             copies.start(f"back{q}{d}", mine, mine, here.along(second, d))
-    copies.wait("hop0")
+    own_sum[0] += ring_end("f0", 0, fine_acc, 0)
+    copies.wait("hop00", "hop01")
     fine_copy = grad_to_out(0, 0, own_sum[0] + hop_in[0].astype(F32), fine_head, fine_grad_out)
     fine_copy.start()
     for q, (first, second, _) in enumerate(ORDERS):
@@ -489,7 +493,7 @@
     for q, (first, _, _) in enumerate(ORDERS):
         mine = (heads, core, q, place[first])
         copies.start(f"share{q}0", mine, mine, here.sibling)
-    copies.wait("hop1")
+    copies.wait("hop10", "hop11")
     coarse_copy = grad_to_out(1, far_rows, own_sum[1] + hop_in[1].astype(F32), coarse_head, coarse_grad_out)
     coarse_copy.start()
     loss_out[...] = loss_round(4, None, None)

time: 104 us -> 101 us (0.971)
  Pallas kernels: 102 us -> 98.9 us
    pallas_call x1, Pallas kernels: 98.1 us -> 94.8 us  [shards(): pl.pallas_call(kernel, out_shape=(jax.ShapeDtypeStruct((8, 128), F32), gr...]
where the time goes in v5:
time: 101 us
  Pallas kernels  98.9 us (98%)
  between operations  1.93 us (2%)
    pallas_call x1, Pallas kernels, shards(): pl.pallas_call(kernel, out_shape=(jax.ShapeDtypeStruct((8, 128), F32), gr...  94.8 us
    pallas_call x1, Pallas kernels, shards(): pl.pallas_call(place, grid=(2,), out_shape=(jax.ShapeDtypeStruct((1,), F3...  4.1 us

profile of v5, /device:TPU:1, one launch (start us, length us, event | category | flops | bytes accessed | tf_op | source)
XLA Modules:
  0.0 100.8 jit_solution(7304646166618337903)
XLA Ops:
  1.9 94.8 %shard_map.101 = (f32[8,128]{1,0:T(8,128)}, f32[192,768]{1,0:T(8,128)}, f32[192,768]{1,0:T(8,128)}, bf16[2,3,4,4,2,48,128]{6,5,4,3,2,1,0:T(8,128)(2,1)}) custom-call(bf16[192,768]{1,0:T(8,128)(2,1)} %fine_rows.1, bf16[192,768]{1,0:T(8,128)(2,1)} %coarse_rows.1, bf16[768,768]{1,0:T(8,128)(2,1)} %fine_head.1, bf16[768,768]{1,0:T(8,128)(2,1)} %coarse_head.1, ...), custom_call_target="tpu_custom_call" | custom-call | flops 21743271936 | bytes 18874368 | tf_op jit(solution)/shard_map/pallas_call | solution.py:575
  96.7 4.1 %shard_map.102 = (f32[1]{0:T(128)}, f32[192,768]{1,0:T(8,128)}, f32[192,768]{1,0:T(8,128)}, f32[768,768]{1,0:T(8,128)}, f32[768,768]{1,0:T(8,128)}) custom-call(f32[8,128]{1,0:T(8,128)} %get-tuple-element.9.refs_0_, f32[192,768]{1,0:T(8,128)} %get-tuple-element.10.refs_1_, f32[192,768]{1,0:T(8,128)} %get-tuple-element.11.refs_2_, ...), custom_call_target="tpu_custom_call" | custom-call | tf_op jit(solution)/shard_map/pallas_call | solution.py:595

commit v6 on v5

--- a/solution.py
+++ b/solution.py
@@ -105,6 +105,7 @@
     unit_keep,
     inv_keep,
     rows_keep,
+    heads_in,
     consts,
     loss_acc,
     sib_out,
@@ -149,16 +150,24 @@
     for device in partners:
         pl.semaphore_signal(barrier, inc=1, device_id=device, device_id_type=MESH)
 
+    loads = [
+        pltpu.make_async_copy(fine_rows, rows_keep.at[0, slot(0)], local_sem.at[4]),
+        pltpu.make_async_copy(coarse_rows, rows_keep.at[1, pl.ds(4 * rows, rows)], local_sem.at[5]),
+        pltpu.make_async_copy(coarse_head, heads_in.at[1], local_sem.at[6]),
+        pltpu.make_async_copy(fine_head, heads_in.at[0], local_sem.at[7]),
+    ]
+    for load in loads:
+        load.start()
+
     consts[0] = 0.5 * jnp.exp(jnp.full((8, width), log_scale[0], F32))
     consts[1] = jnp.full((8, width), 0.5 * bias[0], F32)
     h, shift = consts[0, 0:1, :], consts[1, 0:1, :]
-    inputs = (fine_rows, coarse_rows)
 
     far_rows = 4 * rows
 
     def embed(which, start, keep_unit=False):
         at = pl.ds(start, rows)
-        proj = dot(rows_keep[which, at], (fine_head, coarse_head)[which][...], NN)
+        proj = dot(rows_keep[which, at], heads_in[which], NN)
         inv = lax.rsqrt(jnp.sum(proj * proj, axis=-1, keepdims=True) + EPS)
         unit = proj * inv
         if keep_unit:
@@ -166,8 +175,8 @@
         inv_keep[which, at] = inv
         return unit.astype(BF16)
 
-    rows_keep[0, slot(0)] = fine_rows[...]
-    rows_keep[1, pl.ds(far_rows, rows)] = coarse_rows[...]
+    for i in (0, 1):
+        loads[i].wait()
     pl.semaphore_wait(barrier, len(partners))
     far_device = (here.other_hi, here.other_lo)
 
@@ -207,8 +216,10 @@
     to_far(0, 0, far_rows)
     send_both("fx", "x", rows_keep, 0, (0, 1), (1, 0))
     to_far(1, far_rows, 0)
+    loads[2].wait()
     coarse_all[0, slot(0)] = embed(1, far_rows, True)
     send_both("cy", "y", coarse_all, 0, (0, 1), (1, 0))
+    loads[3].wait()
     fine_all[0, slot(0)] = embed(0, 0, True)
     copies.start("fs", (fine_all, 0, slot(0)), (fine_all, 1, slot(0)), here.sibling)
 
@@ -377,9 +388,9 @@
             for side in (0, 1):
                 dp_keep[which, side, at] = dp[:, side * wide : (side + 1) * wide]
 
-    def grad_to_out(which, start, value, head_ref, out):
+    def grad_to_out(which, start, value, out):
         dp = back(value, unit_keep[which], inv_keep[which, pl.ds(start, rows)])
-        fine_acc[2 * which + 1, slot(0)] = dot(dp, head_ref[...], NT)
+        fine_acc[2 * which + 1, slot(0)] = dot(dp, heads_in[which], NT)
         return pltpu.make_async_copy(fine_acc.at[2 * which + 1, slot(0)], out, local_sem.at[which])
 
     core = here.core
@@ -483,7 +494,7 @@
             copies.start(f"back{q}{d}", mine, mine, here.along(second, d))
     own_sum[0] += ring_end("f0", 0, fine_acc, 0)
     copies.wait("hop00", "hop01")
-    fine_copy = grad_to_out(0, 0, own_sum[0] + hop_in[0].astype(F32), fine_head, fine_grad_out)
+    fine_copy = grad_to_out(0, 0, own_sum[0] + hop_in[0].astype(F32), fine_grad_out)
     fine_copy.start()
     for q, (first, second, _) in enumerate(ORDERS):
         copies.wait(*[f"back{q}{d}" for d in (1, 2, 3)])
@@ -494,7 +505,7 @@
         mine = (heads, core, q, place[first])
         copies.start(f"share{q}0", mine, mine, here.sibling)
     copies.wait("hop10", "hop11")
-    coarse_copy = grad_to_out(1, far_rows, own_sum[1] + hop_in[1].astype(F32), coarse_head, coarse_grad_out)
+    coarse_copy = grad_to_out(1, far_rows, own_sum[1] + hop_in[1].astype(F32), coarse_grad_out)
     coarse_copy.start()
     loss_out[...] = loss_round(4, None, None)
     mine_copy = pltpu.make_async_copy(heads.at[core], heads_out.at[core], local_sem.at[2])
@@ -543,6 +554,7 @@
         VMEM((2, rows, width), F32),
         VMEM((2, 5 * rows, 1), F32),
         VMEM((2, 5 * rows, width), BF16),
+        VMEM((2, width, width), BF16),
         VMEM((2, 8, width), F32),
         VMEM((8, width), F32),
         VMEM((4 * rows, width), BF16),
@@ -566,7 +578,7 @@
         VMEM((4, 4, 8, 128), F32),
         pltpu.SemaphoreType.DMA((N_COPIES,)),
         pltpu.SemaphoreType.DMA((N_COPIES,)),
-        pltpu.SemaphoreType.DMA((4,)),
+        pltpu.SemaphoreType.DMA((8,)),
     ]
     tokens = rows * lax.axis_size("grp") * lax.axis_size("mem")
     pair_flops = 6 * (16 * rows) * (8 * rows) * width
@@ -580,7 +592,7 @@
             grad,
             jax.ShapeDtypeStruct((2, 3, 4, 4, 2, n, 128), BF16),
         ),
-        in_specs=[vmem, vmem, vmem, vmem, smem, smem],
+        in_specs=[anywhere, anywhere, anywhere, anywhere, smem, smem],
         out_specs=(vmem, anywhere, anywhere, anywhere),
         scratch_shapes=scratch,
         cost_estimate=pl.CostEstimate(flops=pair_flops, bytes_accessed=tokens * width, transcendentals=0),
@@ -590,17 +602,17 @@
     def place(*refs):
         place_results(float(tokens) ** 2, *refs)
 
-    by_rows = pl.BlockSpec((rows * 2, width), lambda i: (i, 0))
-    by_halves = pl.BlockSpec((rows // 2, width), lambda i: (i, 0))
+    by_rows = pl.BlockSpec((rows * 4, width), lambda i: (i, 0))
+    by_halves = pl.BlockSpec((rows, width), lambda i: (i, 0))
     return pl.pallas_call(
         place,
-        grid=(2,),
+        grid=(1,),
         out_shape=(jax.ShapeDtypeStruct((1,), F32), grad, grad, head, head),
         in_specs=[
             pl.BlockSpec((8, 128), lambda i: (0, 0)),
             by_halves,
             by_halves,
-            pl.BlockSpec((2, 3, 2, 4, 2, n, 128), lambda i: (0, 0, i, 0, 0, 0, 0)),
+            pl.BlockSpec((2, 3, 4, 4, 2, n, 128), lambda i: (0, 0, i, 0, 0, 0, 0)),
         ],
         out_specs=(smem, by_halves, by_halves, by_rows, by_rows),
     )(loss, fine_grad, coarse_grad, heads)

time: 101 us -> 100 us (0.990)
    pallas_call x1, Pallas kernels: 94.8 us -> 93.2 us  [shards(): pl.pallas_call(kernel, out_shape=(jax.ShapeDtypeStruct((8, 128), F32), gr...]
where the time goes in v6:
time: 100 us; the launch traced here: 99.9 us
  Pallas kernels  97.9 us (98%)
  between operations  2.09 us (2%)
    pallas_call x1, Pallas kernels, shards(): pl.pallas_call(kernel, out_shape=(jax.ShapeDtypeStruct((8, 128), F32), gr...  93.2 us
    pallas_call x1, Pallas kernels, shards(): pl.pallas_call(place, grid=(1,), out_shape=(jax.ShapeDtypeStruct((1,), F3...  4.66 us

profile of v6, /device:TPU:1, one launch (start us, length us, event | category | flops | bytes accessed | tf_op | source)
XLA Modules:
  0.0 99.9 jit_solution(8640264282056103044)
XLA Ops:
  1.9 93.2 %shard_map.101 = (f32[8,128]{1,0:T(8,128)}, f32[192,768]{1,0:T(8,128)}, f32[192,768]{1,0:T(8,128)}, bf16[2,3,4,4,2,48,128]{6,5,4,3,2,1,0:T(8,128)(2,1)}) custom-call(bf16[192,768]{1,0:T(8,128)(2,1)} %fine_rows.1, bf16[192,768]{1,0:T(8,128)(2,1)} %coarse_rows.1, bf16[768,768]{1,0:T(8,128)(2,1)} %fine_head.1, bf16[768,768]{1,0:T(8,128)(2,1)} %coarse_head.1, ...), custom_call_target="tpu_custom_call" | custom-call | flops 21743271936 | bytes 18874368 | tf_op jit(solution)/shard_map/pallas_call | solution.py:587
  95.1 4.7 %shard_map.102 = (f32[1]{0:T(128)}, f32[192,768]{1,0:T(8,128)}, f32[192,768]{1,0:T(8,128)}, f32[768,768]{1,0:T(8,128)}, f32[768,768]{1,0:T(8,128)}) custom-call(f32[8,128]{1,0:T(8,128)} %get-tuple-element.9.refs_0_, f32[192,768]{1,0:T(8,128)} %get-tuple-element.10.refs_1_, f32[192,768]{1,0:T(8,128)} %get-tuple-element.11.refs_2_, ...), custom_call_target="tpu_custom_call" | custom-call | tf_op jit(solution)/shard_map/pallas_call | solution.py:607

commit v7 on v6

--- a/solution.py
+++ b/solution.py
@@ -410,7 +410,7 @@
     value = ring_end("f1", 1, fine_acc, 2)
     hop_out[0] = value.astype(BF16)
     fine_acc[2, slot(0)] = value
-    hop(0, 0, 1)
+    hop(0, 0)
     share_out[1] = dot(rows_keep[1], dp_keep[1, other], TN).astype(BF16)
     keep(0, 0, lambda i, n: fine_acc[0, pl.ds(i, n)] + own_sum[0, pl.ds(i, n)], fine_all, 0, 0)
     keep(0, rows, lambda i, n: fine_acc[0, pl.ds(rows + i, n)], fine_all, 0, rows)
@@ -492,10 +492,7 @@
         mine = (heads, core, q, place[first], place[second])
         for d in (1, 3, 2):
             copies.start(f"back{q}{d}", mine, mine, here.along(second, d))
-    own_sum[0] += ring_end("f0", 0, fine_acc, 0)
-    copies.wait("hop00", "hop01")
-    fine_copy = grad_to_out(0, 0, own_sum[0] + hop_in[0].astype(F32), fine_grad_out)
-    fine_copy.start()
+    hop(0, 1)
     for q, (first, second, _) in enumerate(ORDERS):
         copies.wait(*[f"back{q}{d}" for d in (1, 2, 3)])
         mine = (heads, core, q, place[first])
@@ -504,6 +501,10 @@
     for q, (first, _, _) in enumerate(ORDERS):
         mine = (heads, core, q, place[first])
         copies.start(f"share{q}0", mine, mine, here.sibling)
+    own_sum[0] += ring_end("f0", 0, fine_acc, 0)
+    copies.wait("hop00", "hop01")
+    fine_copy = grad_to_out(0, 0, own_sum[0] + hop_in[0].astype(F32), fine_grad_out)
+    fine_copy.start()
     copies.wait("hop10", "hop11")
     coarse_copy = grad_to_out(1, far_rows, own_sum[1] + hop_in[1].astype(F32), coarse_grad_out)
     coarse_copy.start()

time: 100 us -> 102 us (1.020)
  Pallas kernels: 97.9 us -> 99.4 us
    pallas_call x1, Pallas kernels: 93.2 us -> 94.7 us  [shards(): pl.pallas_call(kernel, out_shape=(jax.ShapeDtypeStruct((8, 128), F32), gr...]
where the time goes in v7:
time: 102 us
  Pallas kernels  99.4 us (97%)
  between operations  2.09 us (2%)
    pallas_call x1, Pallas kernels, shards(): pl.pallas_call(kernel, out_shape=(jax.ShapeDtypeStruct((8, 128), F32), gr...  94.7 us
    pallas_call x1, Pallas kernels, shards(): pl.pallas_call(place, grid=(1,), out_shape=(jax.ShapeDtypeStruct((1,), F3...  4.66 us

profile of v7, /device:TPU:1, one launch (start us, length us, event | category | flops | bytes accessed | tf_op | source)
XLA Modules:
  0.0 101.5 jit_solution(7425121841422541764)
XLA Ops:
  1.9 94.7 %shard_map.101 = (f32[8,128]{1,0:T(8,128)}, f32[192,768]{1,0:T(8,128)}, f32[192,768]{1,0:T(8,128)}, bf16[2,3,4,4,2,48,128]{6,5,4,3,2,1,0:T(8,128)(2,1)}) custom-call(bf16[192,768]{1,0:T(8,128)(2,1)} %fine_rows.1, bf16[192,768]{1,0:T(8,128)(2,1)} %coarse_rows.1, bf16[768,768]{1,0:T(8,128)(2,1)} %fine_head.1, bf16[768,768]{1,0:T(8,128)(2,1)} %coarse_head.1, ...), custom_call_target="tpu_custom_call" | custom-call | flops 21743271936 | bytes 18874368 | tf_op jit(solution)/shard_map/pallas_call | solution.py:588
  96.7 4.7 %shard_map.102 = (f32[1]{0:T(128)}, f32[192,768]{1,0:T(8,128)}, f32[192,768]{1,0:T(8,128)}, f32[768,768]{1,0:T(8,128)}, f32[768,768]{1,0:T(8,128)}) custom-call(f32[8,128]{1,0:T(8,128)} %get-tuple-element.9.refs_0_, f32[192,768]{1,0:T(8,128)} %get-tuple-element.10.refs_1_, f32[192,768]{1,0:T(8,128)} %get-tuple-element.11.refs_2_, ...), custom_call_target="tpu_custom_call" | custom-call | tf_op jit(solution)/shard_map/pallas_call | solution.py:608
